TPU v7x, 128 devices: a whole 4x4x4 slice. The times are simulated.
128 devices in a mesh: seq: 32 (over z, y, core), tp: 4 (over x).
Axes of the slice: x: 4, y: 4, z: 4, core: 2. Of those that a mesh axis runs over, the one named last changes fastest.
Arguments:
- pool_keys: bfloat16 [4096, 16, 1024], P(('seq', 'tp')), may hold values from -6 to 6
- pool_values: bfloat16 [4096, 16, 1024], P(('seq', 'tp')), may hold values from -6 to 6
- passage_ids: int32 [16], replicated, may hold values from 0 to 31, as said below
- page_slot: int32 [32, 128], replicated, may hold values from 0 to 4095, as said below
- offsets: int32 [16], replicated, may hold values from 0 to 33168, as said below
- recompute_blocks: int32 [16, 2], replicated, may hold values from 0 to 15, as said below
- hidden_rows: bfloat16 [4096, 8192], P('seq'), may hold values from -6 to 6
- w_key: bfloat16 [8192, 1024], P(None, 'tp'), may hold values from -0.0625 to 0.0625
- w_value: bfloat16 [8192, 1024], P(None, 'tp'), may hold values from -0.0625 to 0.0625
- queries: bfloat16 [4096, 8192], P('seq', 'tp'), may hold values from -200 to 200
Outputs:
- key_cache: bfloat16 [32768, 1024], P('seq', 'tp')
- value_cache: bfloat16 [32768, 1024], P('seq', 'tp')
- attended: bfloat16 [4096, 8192], P('seq', 'tp')
Inputs may be any that keep to these rules, and one draw needn't show every extreme that they name: `passage_ids`: 16 different pool passage numbers. `page_slot`: every pool slot holds exactly one page. Group the slots by seq index: the slots from s * 2 * 64 on, 128 of them, lie on the devices of seq index s. Among the pages of the passages named in passage_ids, those of one such group that fall on the 1024 tokens of one seq index number at most 4, and the tokens of every seq index receive exactly 4 pages from some group. offsets[0] is below 1024 and each next offset exceeds the one before by 2048 to 2143. `recompute_blocks`: each row holds 2 different block numbers, in rising order.
All inputs are finite; a program needn't handle non-finite values.
Results may differ from a plain program's by a relative error of at most 0.019.
Values may be sent and summed in bfloat16 or wider, within the bound.
A program may use at most 192 MiB of HBM per device.

v0:
```python
import math

import jax
import jax.numpy as jnp
from jax import lax
from jax.sharding import PartitionSpec as P

HD = 128
PASSAGE_LEN = 2048
BLOCK = 128
PAGE = 16
RB = 2
TOK_DEV = 1024


MASKED = -1e30


def frequencies():
    exponent = jnp.arange(0, HD, 2, dtype=jnp.float32) / HD
    base_rate = jnp.power(jnp.float32(500000.0), -exponent)
    wave_length = 2.0 * math.pi / base_rate
    smooth = (8192.0 / wave_length - 1.0) / 3.0
    blended = (1.0 - smooth) * base_rate / 8.0 + smooth * base_rate
    return jnp.where(
        wave_length > 8192.0, base_rate / 8.0, jnp.where(wave_length < 2048.0, base_rate, blended)
    )


def rotate(values, places):
    row_count = values.shape[0]
    rate_table = frequencies()
    angles = places.astype(jnp.float32)[:, None] * rate_table[None, :]
    cosine = jnp.cos(angles)[:, None, :]
    sine_part = jnp.sin(angles)[:, None, :]
    per_head = values.reshape(row_count, -1, HD)
    first_half = per_head[..., : HD // 2]
    second_half = per_head[..., HD // 2 :]
    turned = jnp.concatenate(
        [
            first_half * cosine - second_half * sine_part,
            second_half * cosine + first_half * sine_part,
        ],
        axis=-1,
    )
    return turned.reshape(row_count, -1)


def lookup(small_table, wanted):
    matches = wanted[:, None] == jnp.arange(small_table.shape[0], dtype=jnp.int32)[None, :]
    return jnp.sum(jnp.where(matches, small_table[None, :], 0), axis=1)


def row_places(row_ids, recompute_blocks, offsets):
    passages = recompute_blocks.shape[0]
    passage = row_ids // BLOCK % passages
    which_block = row_ids // (passages * BLOCK)
    in_block = row_ids % BLOCK
    block_start = (
        lookup(recompute_blocks.reshape(-1), passage * RB + which_block) * BLOCK + in_block
    )
    return (passage * PASSAGE_LEN + block_start, lookup(offsets, passage) + block_start)


def token_positions(first_token, offsets):
    token_seq = first_token + jnp.arange(TOK_DEV, dtype=jnp.int32)
    return lookup(offsets, token_seq // PASSAGE_LEN) + token_seq % PASSAGE_LEN


def block_tables(recompute_blocks):
    passages = recompute_blocks.shape[0]
    per_passage = PASSAGE_LEN // BLOCK
    matches = (
        recompute_blocks[:, :, None] == jnp.arange(per_passage, dtype=jnp.int32)[None, None, :]
    )
    numbers = (
        jnp.arange(passages, dtype=jnp.int32)[:, None]
        + jnp.arange(RB, dtype=jnp.int32)[None, :] * passages
    )
    chosen = jnp.any(matches, axis=1).reshape(-1)
    anchor = jnp.sum(jnp.where(matches, numbers[:, :, None], 0), axis=1).reshape(-1)
    return (chosen, anchor)


def blend_rows(base_rows, first_block, fresh_part, tables):
    chosen, anchor = tables
    blocks_here = base_rows.shape[0] // BLOCK
    row_width = base_rows.shape[1]
    picked_flag = lax.dynamic_slice_in_dim(chosen, first_block, blocks_here)
    picked_from = lax.dynamic_slice_in_dim(anchor, first_block, blocks_here)
    replacement = jnp.take(fresh_part.reshape(-1, BLOCK, row_width), picked_from, axis=0)
    merged = jnp.where(
        picked_flag[:, None, None], replacement, base_rows.reshape(blocks_here, BLOCK, row_width)
    )
    return merged.reshape(blocks_here * BLOCK, row_width)


def query_group(query_rows, seen_rows, kv_heads):
    row_count = query_rows.shape[0]
    group_size = query_rows.shape[1] // HD // kv_heads
    grouped = (
        query_rows.reshape(row_count, kv_heads, group_size, HD)
        .transpose(1, 2, 0, 3)
        .reshape(kv_heads, group_size * row_count, HD)
    )
    return (grouped, jnp.tile(seen_rows, group_size), jnp.max(seen_rows))


def empty_state(one_group):
    grouped = one_group[0]
    shape_rows = grouped.shape[:2]
    return (
        jnp.full(shape_rows, MASKED, jnp.float32),
        jnp.zeros(shape_rows, jnp.float32),
        jnp.zeros(grouped.shape, jnp.float32),
    )


def attend_block(carry_in, one_group, key_block, value_block, block_start):
    row_peak, weight_sum, weighted = carry_in
    grouped, seen_rows, last_row = one_group
    key_count = key_block.shape[0]
    kv_heads = grouped.shape[0]
    key_heads = key_block.reshape(key_count, kv_heads, HD)
    value_heads = value_block.reshape(key_count, kv_heads, HD)
    scores = jnp.einsum("hqd,khd->hqk", grouped, key_heads, preferred_element_type=jnp.float32) * (
        1.0 / math.sqrt(HD)
    )
    allowed = (
        seen_rows[None, :, None]
        >= (block_start + jnp.arange(key_count, dtype=jnp.int32))[None, None, :]
    )
    scores = jnp.where(allowed, scores, MASKED)
    new_peak = jnp.maximum(row_peak, jnp.max(scores, axis=2))
    weights = jnp.where(allowed, jnp.exp(scores - new_peak[:, :, None]), 0.0)
    rescale = jnp.exp(row_peak - new_peak)
    weight_sum = weight_sum * rescale + jnp.sum(weights, axis=2)
    weighted = weighted * rescale[:, :, None] + jnp.einsum(
        "hqk,khd->hqd",
        weights.astype(jnp.bfloat16),
        value_heads,
        preferred_element_type=jnp.float32,
    )
    return (new_peak, weight_sum, weighted)


def visit_block(carry_in, one_group, key_block, value_block, block_start):
    return lax.cond(
        block_start <= one_group[2],
        lambda inner_state: attend_block(
            inner_state, one_group, key_block, value_block, block_start
        ),
        lambda inner_state: inner_state,
        carry_in,
    )


def finish_group(carry_in, row_count, kv_heads):
    row_peak, weight_sum, weighted = carry_in
    result = weighted / weight_sum[:, :, None]
    group_size = result.shape[1] // row_count
    return (
        result.reshape(kv_heads, group_size, row_count, HD)
        .transpose(2, 0, 1, 3)
        .reshape(row_count, -1)
        .astype(jnp.bfloat16)
    )


def fold_with(groups, prepare, carry_in, pieces):
    key_rows, value_rows = pieces
    block_count = key_rows.shape[0] // TOK_DEV
    key_blocks = key_rows.reshape(block_count, TOK_DEV, key_rows.shape[1])
    value_blocks = value_rows.reshape(block_count, TOK_DEV, value_rows.shape[1])
    starts = jnp.arange(block_count, dtype=jnp.int32) * TOK_DEV

    def visit_keys(states, scan_item):
        key_block, value_block, block_start = scan_item
        key_block, value_block = prepare(key_block, value_block, block_start)
        updated = tuple(
            (
                visit_block(state_one, one_group, key_block, value_block, block_start)
                for state_one, one_group in zip(states, groups)
            )
        )
        return (updated, None)

    folded, unused = lax.scan(visit_keys, carry_in, (key_blocks, value_blocks, starts))
    return folded


def on_device(
    pool_keys,
    pool_values,
    passage_ids,
    page_slot,
    offsets,
    recompute_blocks,
    hidden_rows,
    w_key,
    w_value,
    queries,
):
    seq_count = lax.axis_size("seq")
    tp_count = lax.axis_size("tp")
    my_index = lax.axis_index("seq")
    pool_dev = pool_keys.shape[0]
    kv_width = pool_keys.shape[2] // tp_count
    kv_heads = kv_width // HD
    per_dest = TOK_DEV // PAGE
    row_pages = tp_count * pool_dev
    capacity = 2 * per_dest // seq_count
    rows_dev = hidden_rows.shape[0]
    used_slots = jnp.take(page_slot, passage_ids, axis=0).reshape(seq_count, per_dest)
    source_row = used_slots // row_pages
    row_local = used_slots % row_pages
    position_ids = jnp.arange(per_dest, dtype=jnp.int32)
    earlier = position_ids[None, :] < position_ids[:, None]
    same_source = source_row[:, :, None] == source_row[:, None, :]
    page_rank = jnp.sum(same_source & earlier[None, :, :], axis=2)
    slot_hit = (source_row == my_index)[:, :, None] & (
        page_rank[:, :, None] == jnp.arange(capacity, dtype=jnp.int32)[None, None, :]
    )
    send_index = jnp.sum(jnp.where(slot_hit, row_local[:, :, None], 0), axis=1).reshape(-1)
    send_live = jnp.any(slot_hit, axis=1)
    split_keys = pool_keys.reshape(pool_dev, PAGE, tp_count, kv_width)
    split_values = pool_values.reshape(pool_dev, PAGE, tp_count, kv_width)
    row_keys, row_values = (
        lax.all_to_all(split_keys, "tp", split_axis=2, concat_axis=0, tiled=True),
        lax.all_to_all(split_values, "tp", split_axis=2, concat_axis=0, tiled=True),
    )

    def outgoing(stacked):
        flat_pages = stacked.reshape(row_pages, PAGE, kv_width)
        picked = jnp.take(flat_pages, send_index, axis=0).reshape(
            seq_count, capacity, PAGE, kv_width
        )
        return jnp.where(send_live[:, :, None, None], picked, jnp.zeros_like(picked))

    got_keys, got_values = (
        lax.all_to_all(outgoing(row_keys), "seq", split_axis=0, concat_axis=0, tiled=True),
        lax.all_to_all(outgoing(row_values), "seq", split_axis=0, concat_axis=0, tiled=True),
    )
    my_source = lax.dynamic_index_in_dim(source_row, my_index, 0, keepdims=False)
    my_rank = lax.dynamic_index_in_dim(page_rank, my_index, 0, keepdims=False)
    arrival = my_source * capacity + my_rank

    def arrived(stacked):
        flat_pages = stacked.reshape(seq_count * capacity, PAGE, kv_width)
        return jnp.take(flat_pages, arrival, axis=0).reshape(TOK_DEV, kv_width)

    cached_keys = arrived(got_keys)
    cached_values = arrived(got_values)
    row_ids = my_index * rows_dev + jnp.arange(rows_dev, dtype=jnp.int32)
    row_seq, row_pos = row_places(row_ids, recompute_blocks, offsets)
    fresh_keys = rotate(
        jnp.dot(hidden_rows, w_key, preferred_element_type=jnp.float32), row_pos
    ).astype(jnp.bfloat16)
    fresh_values = jnp.dot(hidden_rows, w_value, preferred_element_type=jnp.float32).astype(
        jnp.bfloat16
    )
    all_keys, all_values = (
        lax.all_gather(fresh_keys, "seq", axis=0, tiled=True),
        lax.all_gather(fresh_values, "seq", axis=0, tiled=True),
    )
    tables = block_tables(recompute_blocks)
    first_block = my_index * (TOK_DEV // BLOCK)
    token_pos = token_positions(my_index * TOK_DEV, offsets)
    key_cache = blend_rows(
        rotate(cached_keys.astype(jnp.float32), token_pos).astype(jnp.bfloat16),
        first_block,
        all_keys,
        tables,
    )
    value_cache = blend_rows(cached_values, first_block, all_values, tables)
    turned = rotate(queries.astype(jnp.float32), row_pos).astype(jnp.bfloat16)
    row_parts = [(turned, row_seq)]
    groups = tuple(
        (query_group(rows_part, seen_part, kv_heads) for rows_part, seen_part in row_parts)
    )
    starting = tuple((empty_state(one_group) for one_group in groups))

    def prepare(key_block, value_block, block_start):
        return (key_block, value_block)

    folded = fold_with(
        groups,
        prepare,
        starting,
        (
            lax.all_gather(key_cache, "seq", axis=0, tiled=True),
            lax.all_gather(value_cache, "seq", axis=0, tiled=True),
        ),
    )
    outputs = [
        finish_group(state_one, rows_part.shape[0], kv_heads)
        for state_one, (rows_part, seen_part) in zip(folded, row_parts)
    ]
    attended = outputs[0]
    return (key_cache, value_cache, attended)


def solution(mesh):
    placed = (
        P(("seq", "tp"), None, None),
        P(("seq", "tp"), None, None),
        P(),
        P(),
        P(),
        P(),
        P("seq", None),
        P(None, "tp"),
        P(None, "tp"),
        P("seq", "tp"),
    )
    return jax.shard_map(
        on_device,
        mesh=mesh,
        in_specs=placed,
        out_specs=(P("seq", "tp"), P("seq", "tp"), P("seq", "tp")),
        check_vma=False,
    )
```

profile of v0, /device:TPU:121, one launch (start us, length us, event | category | flops | bytes accessed | tf_op | source)
XLA Modules:
  0.0 724.0 jit_solution(9008379036187024384)
XLA Ops:
  65.2 14.2 %all-to-all-done.1 = bf16[32,4,16,256]{3,2,1,0:T(8,128)(2,1)S(1)} async-done(((bf16[32,4,16,256]{3,2,1,0:T(8,128)(2,1)}), bf16[32,4,16,256]{3,2,1,0:T(8,128)(2,1)S(1)}, u32[]{:S(2)}, u32[]{:S(2)}) %all-to-all-start.1) | async-done | bytes 1048608 | tf_op jit(solution)/shard_map/all_to_all | solution.py:241
  90.6 12.2 %all-to-all-done.3 = bf16[32,4,16,256]{3,2,1,0:T(8,128)(2,1)S(1)} async-done(((bf16[32,4,16,256]{3,2,1,0:T(8,128)(2,1)}), bf16[32,4,16,256]{3,2,1,0:T(8,128)(2,1)S(1)}, u32[]{:S(2)}, u32[]{:S(2)}) %all-to-all-start.3) | async-done | bytes 1048608 | tf_op jit(solution)/shard_map/all_to_all | solution.py:242
  116.8 67.0 %all-gather.9.cloned.1.call-done = bf16[32768,256]{1,0:T(8,128)(2,1)} async-done(((bf16[1024,256]{1,0:T(8,128)(2,1)}), bf16[32768,256]{1,0:T(8,128)(2,1)}) %all-gather.9.cloned.1.call-update) | async-done | bytes 16777232 | tf_op jit(solution)/shard_map/all_gather | solution.py:291
  183.8 22.6 %copy.58 = bf16[32,1024,256]{1,2,0:T(8,128)(2,1)} copy(bf16[32,1024,256]{2,1,0:T(8,128)(2,1)} %bitcast.80) | data formatting | bytes 33554432
  206.3 52.2 %all-gather.11.cloned.1.call-done = bf16[32768,256]{1,0:T(8,128)(2,1)} async-done(((bf16[1024,256]{1,0:T(8,128)(2,1)}), bf16[32768,256]{1,0:T(8,128)(2,1)}) %all-gather.11.cloned.1.call-update) | async-done | bytes 16777232 | tf_op jit(solution)/shard_map/all_gather | solution.py:292
  258.5 22.5 %copy.59 = bf16[32,1024,256]{1,2,0:T(8,128)(2,1)} copy(bf16[32,1024,256]{2,1,0:T(8,128)(2,1)} %bitcast.81) | data formatting | bytes 33554432
  281.2 434.7 %while.15 = (s32[]{:T(128)}, f32[2,1024]{1,0:T(2,128)S(1)}, f32[2,1024]{1,0:T(2,128)S(1)}, f32[2,1024,128]{2,1,0:T(8,128)S(1)}, s32[32]{0:T(128)S(1)}, /*index=5...) while((s32[]{:T(128)}, f32[2,1024]{1,0:T(2,128)S(1)}, ...), condition=%wide.region_14.18_spmd.clone, body=%wide.region_9.17_spmd.clone.sunk | while | flops 1102582784 | bytes 35275536 | solution.py:188
  283.1 11.6 %conditional.3 = ((f32[2,1024]{1,0:T(2,128)S(1)}, f32[2,1024]{1,0:T(2,128)S(1)}, f32[2,1024,128]{2,1,0:T(8,128)S(1)})) conditional(s32[]{:T(128)} %convert_element_type.89, (f32[2,1024]{1,0:T(2,128)S(1)}, f32[2,1024]{1,0:T(2,128)S(1)}, f32[2,1024,128]{2,1,0:T(8,128)S(1)}) %tuple.65, (s32[128]{0:T(128)S(1)}, s32[]{:T(128)}, ...), branch_computations={%region_10.13_spmd, %region_11.16_spmd} | conditional | flops 1102582784 | bytes 35275304 | solution.py:148
  296.7 11.6 %conditional.3 = ((f32[2,1024]{1,0:T(2,128)S(1)}, f32[2,1024]{1,0:T(2,128)S(1)}, f32[2,1024,128]{2,1,0:T(8,128)S(1)})) conditional(s32[]{:T(128)} %convert_element_type.89, (f32[2,1024]{1,0:T(2,128)S(1)}, f32[2,1024]{1,0:T(2,128)S(1)}, f32[2,1024,128]{2,1,0:T(8,128)S(1)}) %tuple.65, (s32[128]{0:T(128)S(1)}, s32[]{:T(128)}, ...), branch_computations={%region_10.13_spmd, %region_11.16_spmd} | conditional | flops 1102582784 | bytes 35275304 | solution.py:148
  310.3 11.6 %conditional.3 = ((f32[2,1024]{1,0:T(2,128)S(1)}, f32[2,1024]{1,0:T(2,128)S(1)}, f32[2,1024,128]{2,1,0:T(8,128)S(1)})) conditional(s32[]{:T(128)} %convert_element_type.89, (f32[2,1024]{1,0:T(2,128)S(1)}, f32[2,1024]{1,0:T(2,128)S(1)}, f32[2,1024,128]{2,1,0:T(8,128)S(1)}) %tuple.65, (s32[128]{0:T(128)S(1)}, s32[]{:T(128)}, ...), branch_computations={%region_10.13_spmd, %region_11.16_spmd} | conditional | flops 1102582784 | bytes 35275304 | solution.py:148
  323.9 11.6 %conditional.3 = ((f32[2,1024]{1,0:T(2,128)S(1)}, f32[2,1024]{1,0:T(2,128)S(1)}, f32[2,1024,128]{2,1,0:T(8,128)S(1)})) conditional(s32[]{:T(128)} %convert_element_type.89, (f32[2,1024]{1,0:T(2,128)S(1)}, f32[2,1024]{1,0:T(2,128)S(1)}, f32[2,1024,128]{2,1,0:T(8,128)S(1)}) %tuple.65, (s32[128]{0:T(128)S(1)}, s32[]{:T(128)}, ...), branch_computations={%region_10.13_spmd, %region_11.16_spmd} | conditional | flops 1102582784 | bytes 35275304 | solution.py:148
  337.5 11.6 %conditional.3 = ((f32[2,1024]{1,0:T(2,128)S(1)}, f32[2,1024]{1,0:T(2,128)S(1)}, f32[2,1024,128]{2,1,0:T(8,128)S(1)})) conditional(s32[]{:T(128)} %convert_element_type.89, (f32[2,1024]{1,0:T(2,128)S(1)}, f32[2,1024]{1,0:T(2,128)S(1)}, f32[2,1024,128]{2,1,0:T(8,128)S(1)}) %tuple.65, (s32[128]{0:T(128)S(1)}, s32[]{:T(128)}, ...), branch_computations={%region_10.13_spmd, %region_11.16_spmd} | conditional | flops 1102582784 | bytes 35275304 | solution.py:148
  351.0 11.6 %conditional.3 = ((f32[2,1024]{1,0:T(2,128)S(1)}, f32[2,1024]{1,0:T(2,128)S(1)}, f32[2,1024,128]{2,1,0:T(8,128)S(1)})) conditional(s32[]{:T(128)} %convert_element_type.89, (f32[2,1024]{1,0:T(2,128)S(1)}, f32[2,1024]{1,0:T(2,128)S(1)}, f32[2,1024,128]{2,1,0:T(8,128)S(1)}) %tuple.65, (s32[128]{0:T(128)S(1)}, s32[]{:T(128)}, ...), branch_computations={%region_10.13_spmd, %region_11.16_spmd} | conditional | flops 1102582784 | bytes 35275304 | solution.py:148
  364.6 11.6 %conditional.3 = ((f32[2,1024]{1,0:T(2,128)S(1)}, f32[2,1024]{1,0:T(2,128)S(1)}, f32[2,1024,128]{2,1,0:T(8,128)S(1)})) conditional(s32[]{:T(128)} %convert_element_type.89, (f32[2,1024]{1,0:T(2,128)S(1)}, f32[2,1024]{1,0:T(2,128)S(1)}, f32[2,1024,128]{2,1,0:T(8,128)S(1)}) %tuple.65, (s32[128]{0:T(128)S(1)}, s32[]{:T(128)}, ...), branch_computations={%region_10.13_spmd, %region_11.16_spmd} | conditional | flops 1102582784 | bytes 35275304 | solution.py:148
  378.2 11.6 %conditional.3 = ((f32[2,1024]{1,0:T(2,128)S(1)}, f32[2,1024]{1,0:T(2,128)S(1)}, f32[2,1024,128]{2,1,0:T(8,128)S(1)})) conditional(s32[]{:T(128)} %convert_element_type.89, (f32[2,1024]{1,0:T(2,128)S(1)}, f32[2,1024]{1,0:T(2,128)S(1)}, f32[2,1024,128]{2,1,0:T(8,128)S(1)}) %tuple.65, (s32[128]{0:T(128)S(1)}, s32[]{:T(128)}, ...), branch_computations={%region_10.13_spmd, %region_11.16_spmd} | conditional | flops 1102582784 | bytes 35275304 | solution.py:148
  391.8 11.6 %conditional.3 = ((f32[2,1024]{1,0:T(2,128)S(1)}, f32[2,1024]{1,0:T(2,128)S(1)}, f32[2,1024,128]{2,1,0:T(8,128)S(1)})) conditional(s32[]{:T(128)} %convert_element_type.89, (f32[2,1024]{1,0:T(2,128)S(1)}, f32[2,1024]{1,0:T(2,128)S(1)}, f32[2,1024,128]{2,1,0:T(8,128)S(1)}) %tuple.65, (s32[128]{0:T(128)S(1)}, s32[]{:T(128)}, ...), branch_computations={%region_10.13_spmd, %region_11.16_spmd} | conditional | flops 1102582784 | bytes 35275304 | solution.py:148
  405.4 11.6 %conditional.3 = ((f32[2,1024]{1,0:T(2,128)S(1)}, f32[2,1024]{1,0:T(2,128)S(1)}, f32[2,1024,128]{2,1,0:T(8,128)S(1)})) conditional(s32[]{:T(128)} %convert_element_type.89, (f32[2,1024]{1,0:T(2,128)S(1)}, f32[2,1024]{1,0:T(2,128)S(1)}, f32[2,1024,128]{2,1,0:T(8,128)S(1)}) %tuple.65, (s32[128]{0:T(128)S(1)}, s32[]{:T(128)}, ...), branch_computations={%region_10.13_spmd, %region_11.16_spmd} | conditional | flops 1102582784 | bytes 35275304 | solution.py:148
  419.0 11.6 %conditional.3 = ((f32[2,1024]{1,0:T(2,128)S(1)}, f32[2,1024]{1,0:T(2,128)S(1)}, f32[2,1024,128]{2,1,0:T(8,128)S(1)})) conditional(s32[]{:T(128)} %convert_element_type.89, (f32[2,1024]{1,0:T(2,128)S(1)}, f32[2,1024]{1,0:T(2,128)S(1)}, f32[2,1024,128]{2,1,0:T(8,128)S(1)}) %tuple.65, (s32[128]{0:T(128)S(1)}, s32[]{:T(128)}, ...), branch_computations={%region_10.13_spmd, %region_11.16_spmd} | conditional | flops 1102582784 | bytes 35275304 | solution.py:148
  432.5 11.6 %conditional.3 = ((f32[2,1024]{1,0:T(2,128)S(1)}, f32[2,1024]{1,0:T(2,128)S(1)}, f32[2,1024,128]{2,1,0:T(8,128)S(1)})) conditional(s32[]{:T(128)} %convert_element_type.89, (f32[2,1024]{1,0:T(2,128)S(1)}, f32[2,1024]{1,0:T(2,128)S(1)}, f32[2,1024,128]{2,1,0:T(8,128)S(1)}) %tuple.65, (s32[128]{0:T(128)S(1)}, s32[]{:T(128)}, ...), branch_computations={%region_10.13_spmd, %region_11.16_spmd} | conditional | flops 1102582784 | bytes 35275304 | solution.py:148
  446.1 11.6 %conditional.3 = ((f32[2,1024]{1,0:T(2,128)S(1)}, f32[2,1024]{1,0:T(2,128)S(1)}, f32[2,1024,128]{2,1,0:T(8,128)S(1)})) conditional(s32[]{:T(128)} %convert_element_type.89, (f32[2,1024]{1,0:T(2,128)S(1)}, f32[2,1024]{1,0:T(2,128)S(1)}, f32[2,1024,128]{2,1,0:T(8,128)S(1)}) %tuple.65, (s32[128]{0:T(128)S(1)}, s32[]{:T(128)}, ...), branch_computations={%region_10.13_spmd, %region_11.16_spmd} | conditional | flops 1102582784 | bytes 35275304 | solution.py:148
  459.7 11.6 %conditional.3 = ((f32[2,1024]{1,0:T(2,128)S(1)}, f32[2,1024]{1,0:T(2,128)S(1)}, f32[2,1024,128]{2,1,0:T(8,128)S(1)})) conditional(s32[]{:T(128)} %convert_element_type.89, (f32[2,1024]{1,0:T(2,128)S(1)}, f32[2,1024]{1,0:T(2,128)S(1)}, f32[2,1024,128]{2,1,0:T(8,128)S(1)}) %tuple.65, (s32[128]{0:T(128)S(1)}, s32[]{:T(128)}, ...), branch_computations={%region_10.13_spmd, %region_11.16_spmd} | conditional | flops 1102582784 | bytes 35275304 | solution.py:148
  473.3 11.6 %conditional.3 = ((f32[2,1024]{1,0:T(2,128)S(1)}, f32[2,1024]{1,0:T(2,128)S(1)}, f32[2,1024,128]{2,1,0:T(8,128)S(1)})) conditional(s32[]{:T(128)} %convert_element_type.89, (f32[2,1024]{1,0:T(2,128)S(1)}, f32[2,1024]{1,0:T(2,128)S(1)}, f32[2,1024,128]{2,1,0:T(8,128)S(1)}) %tuple.65, (s32[128]{0:T(128)S(1)}, s32[]{:T(128)}, ...), branch_computations={%region_10.13_spmd, %region_11.16_spmd} | conditional | flops 1102582784 | bytes 35275304 | solution.py:148
  486.9 11.6 %conditional.3 = ((f32[2,1024]{1,0:T(2,128)S(1)}, f32[2,1024]{1,0:T(2,128)S(1)}, f32[2,1024,128]{2,1,0:T(8,128)S(1)})) conditional(s32[]{:T(128)} %convert_element_type.89, (f32[2,1024]{1,0:T(2,128)S(1)}, f32[2,1024]{1,0:T(2,128)S(1)}, f32[2,1024,128]{2,1,0:T(8,128)S(1)}) %tuple.65, (s32[128]{0:T(128)S(1)}, s32[]{:T(128)}, ...), branch_computations={%region_10.13_spmd, %region_11.16_spmd} | conditional | flops 1102582784 | bytes 35275304 | solution.py:148
  500.5 11.6 %conditional.3 = ((f32[2,1024]{1,0:T(2,128)S(1)}, f32[2,1024]{1,0:T(2,128)S(1)}, f32[2,1024,128]{2,1,0:T(8,128)S(1)})) conditional(s32[]{:T(128)} %convert_element_type.89, (f32[2,1024]{1,0:T(2,128)S(1)}, f32[2,1024]{1,0:T(2,128)S(1)}, f32[2,1024,128]{2,1,0:T(8,128)S(1)}) %tuple.65, (s32[128]{0:T(128)S(1)}, s32[]{:T(128)}, ...), branch_computations={%region_10.13_spmd, %region_11.16_spmd} | conditional | flops 1102582784 | bytes 35275304 | solution.py:148
  514.0 11.6 %conditional.3 = ((f32[2,1024]{1,0:T(2,128)S(1)}, f32[2,1024]{1,0:T(2,128)S(1)}, f32[2,1024,128]{2,1,0:T(8,128)S(1)})) conditional(s32[]{:T(128)} %convert_element_type.89, (f32[2,1024]{1,0:T(2,128)S(1)}, f32[2,1024]{1,0:T(2,128)S(1)}, f32[2,1024,128]{2,1,0:T(8,128)S(1)}) %tuple.65, (s32[128]{0:T(128)S(1)}, s32[]{:T(128)}, ...), branch_computations={%region_10.13_spmd, %region_11.16_spmd} | conditional | flops 1102582784 | bytes 35275304 | solution.py:148
  527.6 11.6 %conditional.3 = ((f32[2,1024]{1,0:T(2,128)S(1)}, f32[2,1024]{1,0:T(2,128)S(1)}, f32[2,1024,128]{2,1,0:T(8,128)S(1)})) conditional(s32[]{:T(128)} %convert_element_type.89, (f32[2,1024]{1,0:T(2,128)S(1)}, f32[2,1024]{1,0:T(2,128)S(1)}, f32[2,1024,128]{2,1,0:T(8,128)S(1)}) %tuple.65, (s32[128]{0:T(128)S(1)}, s32[]{:T(128)}, ...), branch_computations={%region_10.13_spmd, %region_11.16_spmd} | conditional | flops 1102582784 | bytes 35275304 | solution.py:148
  541.2 11.6 %conditional.3 = ((f32[2,1024]{1,0:T(2,128)S(1)}, f32[2,1024]{1,0:T(2,128)S(1)}, f32[2,1024,128]{2,1,0:T(8,128)S(1)})) conditional(s32[]{:T(128)} %convert_element_type.89, (f32[2,1024]{1,0:T(2,128)S(1)}, f32[2,1024]{1,0:T(2,128)S(1)}, f32[2,1024,128]{2,1,0:T(8,128)S(1)}) %tuple.65, (s32[128]{0:T(128)S(1)}, s32[]{:T(128)}, ...), branch_computations={%region_10.13_spmd, %region_11.16_spmd} | conditional | flops 1102582784 | bytes 35275304 | solution.py:148
  568.4 11.6 %conditional.3 = ((f32[2,1024]{1,0:T(2,128)S(1)}, f32[2,1024]{1,0:T(2,128)S(1)}, f32[2,1024,128]{2,1,0:T(8,128)S(1)})) conditional(s32[]{:T(128)} %convert_element_type.89, (f32[2,1024]{1,0:T(2,128)S(1)}, f32[2,1024]{1,0:T(2,128)S(1)}, f32[2,1024,128]{2,1,0:T(8,128)S(1)}) %tuple.65, (s32[128]{0:T(128)S(1)}, s32[]{:T(128)}, ...), branch_computations={%region_10.13_spmd, %region_11.16_spmd} | conditional | flops 1102582784 | bytes 35275304 | solution.py:148
  582.0 11.6 %conditional.3 = ((f32[2,1024]{1,0:T(2,128)S(1)}, f32[2,1024]{1,0:T(2,128)S(1)}, f32[2,1024,128]{2,1,0:T(8,128)S(1)})) conditional(s32[]{:T(128)} %convert_element_type.89, (f32[2,1024]{1,0:T(2,128)S(1)}, f32[2,1024]{1,0:T(2,128)S(1)}, f32[2,1024,128]{2,1,0:T(8,128)S(1)}) %tuple.65, (s32[128]{0:T(128)S(1)}, s32[]{:T(128)}, ...), branch_computations={%region_10.13_spmd, %region_11.16_spmd} | conditional | flops 1102582784 | bytes 35275304 | solution.py:148
  595.5 11.6 %conditional.3 = ((f32[2,1024]{1,0:T(2,128)S(1)}, f32[2,1024]{1,0:T(2,128)S(1)}, f32[2,1024,128]{2,1,0:T(8,128)S(1)})) conditional(s32[]{:T(128)} %convert_element_type.89, (f32[2,1024]{1,0:T(2,128)S(1)}, f32[2,1024]{1,0:T(2,128)S(1)}, f32[2,1024,128]{2,1,0:T(8,128)S(1)}) %tuple.65, (s32[128]{0:T(128)S(1)}, s32[]{:T(128)}, ...), branch_computations={%region_10.13_spmd, %region_11.16_spmd} | conditional | flops 1102582784 | bytes 35275304 | solution.py:148
  609.1 11.6 %conditional.3 = ((f32[2,1024]{1,0:T(2,128)S(1)}, f32[2,1024]{1,0:T(2,128)S(1)}, f32[2,1024,128]{2,1,0:T(8,128)S(1)})) conditional(s32[]{:T(128)} %convert_element_type.89, (f32[2,1024]{1,0:T(2,128)S(1)}, f32[2,1024]{1,0:T(2,128)S(1)}, f32[2,1024,128]{2,1,0:T(8,128)S(1)}) %tuple.65, (s32[128]{0:T(128)S(1)}, s32[]{:T(128)}, ...), branch_computations={%region_10.13_spmd, %region_11.16_spmd} | conditional | flops 1102582784 | bytes 35275304 | solution.py:148
  704.2 11.6 %conditional.3 = ((f32[2,1024]{1,0:T(2,128)S(1)}, f32[2,1024]{1,0:T(2,128)S(1)}, f32[2,1024,128]{2,1,0:T(8,128)S(1)})) conditional(s32[]{:T(128)} %convert_element_type.89, (f32[2,1024]{1,0:T(2,128)S(1)}, f32[2,1024]{1,0:T(2,128)S(1)}, f32[2,1024,128]{2,1,0:T(8,128)S(1)}) %tuple.65, (s32[128]{0:T(128)S(1)}, s32[]{:T(128)}, ...), branch_computations={%region_10.13_spmd, %region_11.16_spmd} | conditional | flops 1102582784 | bytes 35275304 | solution.py:148
  (470 shorter events, 555.1 us)
Async XLA Ops:
  7.2 2.0 copy-start
  7.2 7.2 copy-start.3
  7.2 101.4 %all-gather.5.cloned.1.call-start = ((), (), s32[]{:S(2)}) async-start(), calls=%async_computation.4 | async-start | bytes 2162688 | tf_op jit(solution)/shard_map/all_gather | solution.py:263
  9.1 13.9 %copy-start.8 = (s32[16]{0:T(128)S(1)}, s32[16]{0:T(128)}, u32[]{:S(2)}) copy-start(s32[16]{0:T(128)} %param.22) | copy-start | bytes 196
  9.1 13.9 %copy-start.5 = (s32[32,128]{1,0:T(8,128)S(1)}, s32[32,128]{1,0:T(8,128)}, u32[]{:S(2)}) copy-start(s32[32,128]{1,0:T(8,128)} %param.23) | copy-start | bytes 49156
  15.4 18.2 %all-to-all-start.2 = ((bf16[32,16,4,256]{3,1,0,2:T(8,128)(2,1)}), bf16[32,16,4,256]{3,1,0,2:T(8,128)(2,1)S(1)}, u32[]{:S(2)}, u32[]{:S(2)}) async-start(bf16[32,16,4,256]{3,1,0,2:T(8,128)(2,1)} %bitcast.89), calls=%async_computation.2 | async-start | bytes 2097152 | tf_op jit(solution)/shard_map/all_to_all | solution.py:230
  19.5 91.4 %all-gather.7.cloned.1.call-start = ((), (), s32[]{:S(2)}) async-start(), calls=%async_computation.5 | async-start | bytes 2162688 | tf_op jit(solution)/shard_map/all_gather | solution.py:264
  33.6 4.3 copy-start.2
  33.6 31.1 %copy-start.6 = (s32[16,2]{0,1:T(2,128)S(1)}, s32[16,2]{0,1:T(2,128)}, u32[]{:S(2)}) copy-start(s32[16,2]{0,1:T(2,128)} %param.25) | copy-start | bytes 388
  33.6 16.9 %all-to-all-start = ((bf16[32,16,4,256]{3,1,0,2:T(8,128)(2,1)}), bf16[32,16,4,256]{3,1,0,2:T(8,128)(2,1)S(1)}, u32[]{:S(2)}, u32[]{:S(2)}) async-start(bf16[32,16,4,256]{3,1,0,2:T(8,128)(2,1)} %bitcast.74), calls=%async_computation | async-start | bytes 2097152 | tf_op jit(solution)/shard_map/all_to_all | solution.py:229
  38.0 48.9 %copy-start.7 = (s32[16]{0:T(128)S(1)}, s32[16]{0:T(128)}, u32[]{:S(2)}) copy-start(s32[16]{0:T(128)} %param.24) | copy-start | bytes 196
  55.2 24.2 %all-to-all-start.1 = ((bf16[32,4,16,256]{3,2,1,0:T(8,128)(2,1)}), bf16[32,4,16,256]{3,2,1,0:T(8,128)(2,1)S(1)}, u32[]{:S(2)}, u32[]{:S(2)}) async-start(bf16[32,4,16,256]{3,2,1,0:T(8,128)(2,1)} %get-tuple-element.255), calls=%async_computation.1 | async-start | bytes 2097152 | tf_op jit(solution)/shard_map/all_to_all | solution.py:241
  79.4 23.4 %all-to-all-start.3 = ((bf16[32,4,16,256]{3,2,1,0:T(8,128)(2,1)}), bf16[32,4,16,256]{3,2,1,0:T(8,128)(2,1)S(1)}, u32[]{:S(2)}, u32[]{:S(2)}) async-start(bf16[32,4,16,256]{3,2,1,0:T(8,128)(2,1)} %get-tuple-element.254), calls=%async_computation.3 | async-start | bytes 2097152 | tf_op jit(solution)/shard_map/all_to_all | solution.py:242
  86.7 97.1 %all-gather.9.cloned.1.call-start = ((), (), s32[]{:S(2)}) async-start(), calls=%async_computation.6 | async-start | bytes 17301504 | tf_op jit(solution)/shard_map/all_gather | solution.py:291
  103.6 11.2 %copy-start.4 = (bf16[128,2048]{1,0:T(8,128)(2,1)S(1)}, bf16[128,2048]{1,0:T(8,128)(2,1)}, u32[]{:S(2)}) copy-start(bf16[128,2048]{1,0:T(8,128)(2,1)} %param.29) | copy-start | bytes 1572868
  114.2 144.3 %all-gather.11.cloned.1.call-start = ((), (), s32[]{:S(2)}) async-start(), calls=%async_computation.7 | async-start | bytes 17301504 | tf_op jit(solution)/shard_map/all_gather | solution.py:292
  715.8 1.6 copy-start.1
Sparse Core Ops, SparseCore 0:
  14.5 42.9 all-gather.4
  60.3 49.4 all-gather.6
  114.3 69.4 all-gather.8
  186.5 71.9 all-gather.10
where the time goes:
time: 730 us; the launch traced here: 724 us
  matrix products  220 us (30%)
  waiting for transfers between devices  163 us (22%)
  other arithmetic  131 us (18%)
  local copies, waits for them, and re-layouts  126 us (17%)
  loops' own time  45.2 us (6%)
  starting transfers between devices  24.6 us (3%)
  between operations  14.2 us (2%)
    dot_general x32, matrix products, attend_block(): jnp.einsum('hqk,khd->hqd', weights.astype(jnp.bfloat16), value_heads, pre...  118 us
    dot_general x32, matrix products, attend_block(): jnp.einsum('hqd,khd->hqk', grouped, key_heads, preferred_element_type=jnp...  96.1 us
    reduce_sum x32, other arithmetic, attend_block(): weight_sum = weight_sum * rescale + jnp.sum(weights, axis=2)  72.3 us
    all_gather x1, waiting for transfers between devices, on_device(): lax.all_gather(key_cache, 'seq', axis=0, tiled=True)  67 us
    dynamic_slice x64, local copies, waits for them, and re-layouts, fold_with(): lax.scan(visit_keys, carry_in, (key_blocks, value_blocks, starts))  61.4 us
    all_gather x1, waiting for transfers between devices, on_device(): lax.all_gather(value_cache, 'seq', axis=0, tiled=True)  52.2 us
    unnamed x24, local copies, waits for them, and re-layouts  47.8 us
    another operation x1, loops' own time, fold_with(): lax.scan(visit_keys, carry_in, (key_blocks, value_blocks, starts))  43 us
  transfers between devices with their start and end apart: 8, of which 6 were waited for; matrix products, arithmetic and copies ran while one was open for 7% of the time, Pallas kernels for 0%

commit v1 on v0

v1 whole, which is shorter than its diff:
```python
import math

import jax
import jax.numpy as jnp
from jax import lax
from jax.experimental import pallas as pl
from jax.experimental.pallas import tpu as pltpu
from jax.sharding import PartitionSpec as P

HD = 128
PASSAGE_LEN = 2048
BLOCK = 128
PAGE = 16
RB = 2
TOK_DEV = 1024
CAP = 4
N_SEQ = 32
N_TP = 4
PASSAGES = 16
PER_DEST = TOK_DEV // PAGE
WIDTH = 256
HEADS = 16
MASKED = -1e30
EXPONENT = math.log2(math.e) / math.sqrt(HD)
QT = 256
UNIT = QT // BLOCK
BY_KEY = (((1,), (1,)), ((), ()))
MESH = pl.DeviceIdType.MESH


def frequencies():
    exponent = jnp.arange(0, HD, 2, dtype=jnp.float32) / HD
    base_rate = jnp.power(jnp.float32(500000.0), -exponent)
    wave_length = 2.0 * math.pi / base_rate
    smooth = (8192.0 / wave_length - 1.0) / 3.0
    blended = (1.0 - smooth) * base_rate / 8.0 + smooth * base_rate
    return jnp.where(
        wave_length > 8192.0, base_rate / 8.0, jnp.where(wave_length < 2048.0, base_rate, blended)
    )


def tables_at(places):
    rates = frequencies()
    angles = places.astype(jnp.float32)[:, None] * jnp.concatenate([rates, rates])[None, :]
    sign = jnp.where(jnp.arange(HD) < HD // 2, -1.0, 1.0).astype(jnp.float32)
    return jnp.cos(angles), jnp.sin(angles) * sign[None, :]


def lookup(small_table, wanted):
    matches = wanted[:, None] == jnp.arange(small_table.shape[0], dtype=jnp.int32)[None, :]
    return jnp.sum(jnp.where(matches, small_table[None, :], 0), axis=1)


def row_places(row_ids, recompute_blocks, offsets):
    passage = row_ids // BLOCK % PASSAGES
    which_block = row_ids // (PASSAGES * BLOCK)
    block_start = (
        lookup(recompute_blocks.reshape(-1), passage * RB + which_block) * BLOCK + row_ids % BLOCK
    )
    return lookup(offsets, passage) + block_start


def token_positions(first_token, offsets):
    token_seq = first_token + jnp.arange(TOK_DEV, dtype=jnp.int32)
    return lookup(offsets, token_seq // PASSAGE_LEN) + token_seq % PASSAGE_LEN


def turn(values, cosine, sine):
    return values * cosine + pltpu.roll(values, HD // 2, 1) * sine


def on_seq(source, target, send_sem, recv_sem, peer):
    return pltpu.make_async_remote_copy(
        src_ref=source,
        dst_ref=target,
        send_sem=send_sem,
        recv_sem=recv_sem,
        device_id={"seq": peer},
        device_id_type=MESH,
    )


def place(me):
    z = me // 8
    return z, (me // 2) % 4, me % 2, z % 2


def exchange_kernel(
    send_index, arrival, blend,
    pool_k, pool_v, fresh, queries, q_cos, q_sin, t_cos, t_sin,
    out_k, out_v, out_q,
    rows_k, rows_v, outgoing, arriving_k, arriving_v, turned, fresh_in,
    own_sem, tp_send, tp_recv, page_send, page_recv, q_send, q_recv, f_send, f_recv,
):
    me = lax.axis_index("seq")
    my_tp = lax.axis_index("tp")
    z, y, core, half = place(me)
    barrier = pltpu.get_barrier_semaphore()

    def greet_seq(step, _):
        pl.semaphore_signal(
            barrier, inc=1, device_id={"seq": lax.rem(me + step, N_SEQ)}, device_id_type=MESH
        )
        return 0

    lax.fori_loop(1, N_SEQ, greet_seq, 0)
    for step in range(1, N_TP):
        pl.semaphore_signal(
            barrier, inc=1, device_id={"tp": lax.rem(my_tp + step, N_TP)}, device_id_type=MESH
        )
    pl.semaphore_wait(barrier, N_SEQ - 1 + N_TP - 1)

    pools = (pool_k, pool_v)
    rows = (rows_k, rows_v)
    arriving = (arriving_k, arriving_v)

    def columns(which, owner):
        return pools[which].at[:, :, pl.ds(pl.multiple_of(owner * WIDTH, WIDTH), WIDTH)]

    def tp_copy(which, step):
        peer = lax.rem(my_tp + step, N_TP)
        return pltpu.make_async_remote_copy(
            src_ref=columns(which, peer),
            dst_ref=rows[which].at[pl.ds(my_tp * 32, 32)],
            send_sem=tp_send.at[which, step],
            recv_sem=tp_recv.at[which, step],
            device_id={"tp": peer},
            device_id_type=MESH,
        )

    def own_copy(which):
        return pltpu.make_async_copy(
            columns(which, my_tp), rows[which].at[pl.ds(my_tp * 32, 32)], own_sem.at[which]
        )

    for which in range(2):
        for step in (1, 3, 2):
            tp_copy(which, step).start()
        own_copy(which).start()

    for head in range(HEADS):
        cols = slice(head * HD, (head + 1) * HD)
        turned[head] = turn(
            queries[:, cols].astype(jnp.float32), q_cos[...], q_sin[...]
        ).astype(jnp.bfloat16)
    group_z = z - half + lax.rem(half + y // 2, 2)

    def q_dest(other_y):
        return group_z * 8 + other_y * 2 + core

    def q_remote(other_y):
        return on_seq(
            turned, out_q.at[y], q_send.at[other_y], q_recv.at[y], q_dest(other_y)
        )

    def q_local():
        return pltpu.make_async_copy(turned, out_q.at[y], q_recv.at[y])

    which_block = me // PASSAGES
    home = lax.rem(me, PASSAGES) * 2

    def f_remote(side):
        return on_seq(
            fresh, fresh_in.at[which_block], f_send.at[side], f_recv.at[which_block], home + side
        )

    def f_local():
        return pltpu.make_async_copy(fresh, fresh_in.at[which_block], f_recv.at[which_block])

    for side in range(2):

        @pl.when(home + side != me)
        def _():
            f_remote(side).start()

        @pl.when(home + side == me)
        def _():
            f_local().start()

    for other_y in range(4):

        @pl.when(q_dest(other_y) != me)
        def _():
            q_remote(other_y).start()

        @pl.when(q_dest(other_y) == me)
        def _():
            q_local().start()

    def page_copy(which, step):
        peer = lax.rem(me + step, N_SEQ)
        return on_seq(
            outgoing.at[which, peer],
            arriving[which].at[me],
            page_send.at[which, step],
            page_recv.at[which, step],
            peer,
        )

    for which in range(2):
        for step in range(1, N_TP):
            peer = lax.rem(my_tp + N_TP - step, N_TP)
            pltpu.make_async_remote_copy(
                src_ref=columns(which, my_tp),
                dst_ref=rows[which].at[pl.ds(peer * 32, 32)],
                send_sem=tp_send.at[which, step],
                recv_sem=tp_recv.at[which, step],
                device_id={"tp": peer},
                device_id_type=MESH,
            ).wait_recv()
        own_copy(which).wait()

        def pick(step, _):
            peer = lax.rem(me + step, N_SEQ)
            for rank in range(CAP):
                outgoing[which, peer, rank] = rows[which][send_index[peer * CAP + rank]]

            @pl.when(step > 0)
            def _():
                page_copy(which, step).start()

            return 0

        lax.fori_loop(0, N_SEQ, pick, 0)
        arriving[which][me] = outgoing[which, me]

    for slot in range(4):
        on_seq(turned, out_q.at[slot], q_send.at[0], q_recv.at[slot], me).wait_recv()
    for slot in range(2):
        on_seq(fresh, fresh_in.at[slot], f_send.at[0], f_recv.at[slot], me).wait_recv()

    for which in range(2):

        def landed(step, _):
            sender = lax.rem(me + N_SEQ - step, N_SEQ)
            on_seq(
                outgoing.at[which, me],
                arriving[which].at[sender],
                page_send.at[which, step],
                page_recv.at[which, step],
                sender,
            ).wait_recv()
            return 0

        lax.fori_loop(1, N_SEQ, landed, 0)

        def put(page, _):
            slot = arrival[page]
            block = page // 8
            where = pl.ds(pl.multiple_of(page * PAGE, PAGE), PAGE)
            within = pl.ds(pl.multiple_of(lax.rem(page, 8) * PAGE, PAGE), PAGE)
            got = arriving[which][slot // CAP, lax.rem(slot, CAP)]
            if which == 0:
                wide = got.astype(jnp.float32)
                cosine, sine = t_cos[where], t_sin[where]
                got = jnp.concatenate(
                    [
                        turn(wide[:, :HD], cosine, sine).astype(jnp.bfloat16),
                        turn(wide[:, HD:], cosine, sine).astype(jnp.bfloat16),
                    ],
                    axis=1,
                )
            new = fresh_in[blend[1, block], which, within]
            flag = jnp.full(got.shape, blend[0, block], jnp.int32) > 0
            mixed = jnp.where(flag, new.astype(jnp.float32), got.astype(jnp.float32))
            (out_k, out_v)[which][where] = mixed.astype(jnp.bfloat16)
            return 0

        lax.fori_loop(0, PER_DEST, put, 0)

    for which in range(2):
        for step in range(1, N_TP):
            tp_copy(which, step).wait_send()

        def sent(step, _):
            page_copy(which, step).wait_send()
            return 0

        lax.fori_loop(1, N_SEQ, sent, 0)
    for other_y in range(4):

        @pl.when(q_dest(other_y) != me)
        def _():
            q_remote(other_y).wait_send()

    for side in range(2):

        @pl.when(home + side != me)
        def _():
            f_remote(side).wait_send()


def attend_kernel(
    starts,
    own_k, own_v, q_ref,
    out_ref,
    k_buf, v_buf, acc, peak, part, stat, part_in, stat_in,
    own_sem, kv_send, kv_recv, side_send, side_recv, part_send, part_recv,
):
    me = lax.axis_index("seq")
    z, y, core, half = place(me)
    pair = z - half
    sibling = me + 1 - 2 * core
    barrier = pltpu.get_barrier_semaphore()

    def greet(step, _):
        pl.semaphore_signal(
            barrier, inc=1, device_id={"seq": lax.rem(me + step, N_SEQ)}, device_id_type=MESH
        )
        return 0

    lax.fori_loop(1, N_SEQ, greet, 0)
    pl.semaphore_wait(barrier, N_SEQ - 1)

    owns = (own_k, own_v)
    bufs = (k_buf, v_buf)

    def near(step):
        return lax.rem(z + step, 4)

    def at(level):
        return level * 8 + y * 2 + core

    def own_copy(which):
        return pltpu.make_async_copy(owns[which], bufs[which].at[z, core], own_sem.at[which])

    def kv_copy(which, step):
        return on_seq(
            owns[which], bufs[which].at[z, core], kv_send.at[which, step],
            kv_recv.at[which, step], at(near(step)),
        )

    def kv_landed(which, step):
        level = near(4 - step)
        return on_seq(
            owns[which], bufs[which].at[level, core], kv_send.at[which, step],
            kv_recv.at[which, step], at(level),
        )

    def side_copy(which, step):
        level = near(4 - step) if step else z
        source = bufs[which].at[level, core] if step else owns[which]
        return on_seq(
            source, bufs[which].at[level, core], side_send.at[which, step],
            side_recv.at[which, step], sibling,
        )

    def side_landed(which, step):
        level = near(4 - step) if step else z
        return on_seq(
            owns[which], bufs[which].at[level, 1 - core], side_send.at[which, step],
            side_recv.at[which, step], sibling,
        )

    for which in range(2):
        side_copy(which, 0).start()
        own_copy(which).start()
    for step in (1, 3, 2):
        for which in range(2):
            kv_copy(which, step).start()
    acc[...] = jnp.zeros_like(acc)
    peak[...] = jnp.full_like(peak, MASKED)

    ones = jnp.ones((PASSAGE_LEN, HD), jnp.bfloat16)

    def fold(slot, level, limit):
        def unit(index, _):
            for group in range(2):
                cols = slice(group * HD, (group + 1) * HD)
                heads = pl.ds(group * 8 + index * UNIT, UNIT)
                q = q_ref[slot, heads].reshape(QT, HD)
                keys = k_buf[level].reshape(PASSAGE_LEN, WIDTH)[:, cols]
                values = v_buf[level].reshape(PASSAGE_LEN, WIDTH)[:, cols]
                score = lax.dot_general(q, keys, BY_KEY, preferred_element_type=jnp.float32)
                if limit is not None:
                    token = lax.broadcasted_iota(jnp.int32, score.shape, 1)
                    row = lax.broadcasted_iota(jnp.int32, score.shape, 0) % BLOCK + limit
                    allowed = token <= row
                    score = jnp.where(allowed, score, MASKED)
                old = peak[slot, heads].reshape(QT, HD)
                new = jnp.maximum(old, jnp.max(score, axis=1, keepdims=True))
                keep = jnp.exp2((old - new) * EXPONENT)
                weight = jnp.exp2((score - new[:, :1]) * EXPONENT).astype(jnp.bfloat16)
                total = jnp.dot(
                    weight,
                    jnp.concatenate([values, ones], axis=1),
                    preferred_element_type=jnp.float32,
                )
                before = acc[slot, heads].reshape(QT, 2 * HD)
                acc[slot, heads] = (before * keep[:, :1] + total).reshape(UNIT, BLOCK, 2 * HD)
                peak[slot, heads] = new.reshape(UNIT, BLOCK, HD)
            return 0

        lax.fori_loop(0, 8 // UNIT, unit, 0)

    def slot_passage(slot):
        return lax.rem(half + slot // 2, 2) * 8 + 2 * slot + core

    def visit(slot, level):
        passage = level * 4 + y
        mine = slot_passage(slot)

        @pl.when(passage < mine)
        def _():
            fold(slot, level, None)

        @pl.when(passage == mine)
        def _():
            fold(slot, level, starts[slot])

    def owner(slot):
        return (pair + lax.rem(half + slot // 2, 2)) * 8 + slot * 2 + core

    def part_copies(slot):
        return (
            on_seq(part.at[slot], part_in.at[y], part_send.at[0, slot], part_recv.at[0, y],
                   owner(slot)),
            on_seq(stat.at[slot], stat_in.at[y], part_send.at[1, slot], part_recv.at[1, y],
                   owner(slot)),
        )

    def local_copies(slot):
        return (
            pltpu.make_async_copy(part.at[slot], part_in.at[y], part_recv.at[0, y]),
            pltpu.make_async_copy(stat.at[slot], stat_in.at[y], part_recv.at[1, y]),
        )

    def give_back(slot):
        lane = lax.broadcasted_iota(jnp.int32, (BLOCK, HD), 1)

        def head_part(head, logs):
            total = acc[slot, head]
            weight_sum = total[:, HD:]
            some = weight_sum > 0.0
            safe = jnp.where(some, weight_sum, 1.0)
            part[slot, head] = (total[:, :HD] / safe).astype(jnp.bfloat16)
            size = jnp.where(some, peak[slot, head] * EXPONENT + jnp.log2(safe), MASKED)
            return jnp.where(lane == head, size, logs)

        stat[slot] = lax.fori_loop(
            0, HEADS, head_part, jnp.full((BLOCK, HD), MASKED, jnp.float32)
        )

        @pl.when(owner(slot) != me)
        def _():
            for copy in part_copies(slot):
                copy.start()

        @pl.when(owner(slot) == me)
        def _():
            for copy in local_copies(slot):
                copy.start()

    for step in (0, 1, 3, 2):
        level = near(4 - step) if step else z
        for which in range(2):
            if step:
                kv_landed(which, step).wait_recv()
                side_copy(which, step).start()
            else:
                own_copy(which).wait()
        for which in range(2):
            side_landed(which, step).wait_recv()

        def each(slot, _):
            visit(slot, level)
            if step == 2:
                give_back(slot)
            return 0

        lax.fori_loop(0, 4, each, 0)

    for slot in range(4):
        on_seq(part.at[0], part_in.at[slot], part_send.at[0, 0], part_recv.at[0, slot],
               me).wait_recv()
        on_seq(stat.at[0], stat_in.at[slot], part_send.at[1, 0], part_recv.at[1, slot],
               me).wait_recv()
    logs = [stat_in[slot] for slot in range(4)]
    top = jnp.maximum(jnp.maximum(logs[0], logs[1]), jnp.maximum(logs[2], logs[3]))
    shares = [jnp.exp2(log - top) for log in logs]
    whole = 1.0 / (shares[0] + shares[1] + shares[2] + shares[3])
    shares = [share * whole for share in shares]
    for head in range(HEADS):
        result = sum(
            part_in[slot, head].astype(jnp.float32) * shares[slot][:, head : head + 1]
            for slot in range(4)
        )
        out_ref[:, head * HD : (head + 1) * HD] = result.astype(jnp.bfloat16)

    for which in range(2):
        for step in (1, 3, 2):
            kv_copy(which, step).wait_send()
        for step in range(4):
            side_copy(which, step).wait_send()
    for slot in range(4):

        @pl.when(owner(slot) != me)
        def _():
            for copy in part_copies(slot):
                copy.wait_send()


def on_device(
    pool_keys,
    pool_values,
    passage_ids,
    page_slot,
    offsets,
    recompute_blocks,
    hidden_rows,
    w_key,
    w_value,
    queries,
):
    me = lax.axis_index("seq")
    row_pages = N_TP * pool_keys.shape[0]
    used_slots = jnp.take(page_slot, passage_ids, axis=0).reshape(N_SEQ, PER_DEST)
    source_row = used_slots // row_pages
    row_local = used_slots % row_pages
    position_ids = jnp.arange(PER_DEST, dtype=jnp.int32)
    earlier = position_ids[None, :] < position_ids[:, None]
    same_source = source_row[:, :, None] == source_row[:, None, :]
    page_rank = jnp.sum(same_source & earlier[None, :, :], axis=2)
    slot_hit = (source_row == me)[:, :, None] & (
        page_rank[:, :, None] == jnp.arange(CAP, dtype=jnp.int32)[None, None, :]
    )
    send_index = jnp.sum(jnp.where(slot_hit, row_local[:, :, None], 0), axis=1).reshape(-1)
    my_source = lax.dynamic_index_in_dim(source_row, me, 0, keepdims=False)
    my_rank = lax.dynamic_index_in_dim(page_rank, me, 0, keepdims=False)
    arrival = my_source * CAP + my_rank

    passage = me // 2
    blocks = lax.dynamic_index_in_dim(recompute_blocks, passage, 0, keepdims=False)
    here = (me % 2) * 8 + jnp.arange(8, dtype=jnp.int32)
    hit = blocks[:, None] == here[None, :]
    blend = jnp.stack([jnp.any(hit, axis=0).astype(jnp.int32), hit[1].astype(jnp.int32)])

    row_pos = row_places(me * BLOCK + jnp.arange(BLOCK, dtype=jnp.int32), recompute_blocks, offsets)
    token_pos = token_positions(me * TOK_DEV, offsets)
    cosine, sine = tables_at(jnp.concatenate([row_pos, token_pos]))
    q_cos, t_cos = cosine[:BLOCK], cosine[BLOCK:]
    q_sin, t_sin = sine[:BLOCK], sine[BLOCK:]
    raw = jnp.dot(hidden_rows, w_key, preferred_element_type=jnp.float32).reshape(BLOCK, 2, HD)
    swapped = jnp.concatenate([raw[..., HD // 2 :], raw[..., : HD // 2]], axis=-1)
    fresh_keys = (raw * q_cos[:, None, :] + swapped * q_sin[:, None, :]).astype(jnp.bfloat16)
    fresh_values = jnp.dot(hidden_rows, w_value, preferred_element_type=jnp.float32).astype(
        jnp.bfloat16
    )
    fresh = jnp.stack([fresh_keys.reshape(BLOCK, WIDTH), fresh_values])

    vmem = pl.BlockSpec(memory_space=pltpu.VMEM)
    smem = pl.BlockSpec(memory_space=pltpu.SMEM)
    hbm = pl.BlockSpec(memory_space=pl.ANY)
    bf16 = jnp.bfloat16
    dma = pltpu.SemaphoreType.DMA
    key_cache, value_cache, q_group = pl.pallas_call(
        exchange_kernel,
        out_shape=[
            jax.ShapeDtypeStruct((TOK_DEV, WIDTH), bf16),
            jax.ShapeDtypeStruct((TOK_DEV, WIDTH), bf16),
            jax.ShapeDtypeStruct((4, HEADS, BLOCK, HD), bf16),
        ],
        in_specs=[smem, smem, smem, hbm, hbm, vmem, vmem, vmem, vmem, vmem, vmem],
        out_specs=[vmem, vmem, hbm],
        scratch_shapes=[
            pltpu.VMEM((128, PAGE, WIDTH), bf16),
            pltpu.VMEM((128, PAGE, WIDTH), bf16),
            pltpu.VMEM((2, N_SEQ, CAP, PAGE, WIDTH), bf16),
            pltpu.VMEM((N_SEQ, CAP, PAGE, WIDTH), bf16),
            pltpu.VMEM((N_SEQ, CAP, PAGE, WIDTH), bf16),
            pltpu.VMEM((HEADS, BLOCK, HD), bf16),
            pltpu.VMEM((RB, 2, BLOCK, WIDTH), bf16),
            dma((2,)),
            dma((2, N_TP)),
            dma((2, N_TP)),
            dma((2, N_SEQ)),
            dma((2, N_SEQ)),
            dma((4,)),
            dma((4,)),
            dma((2,)),
            dma((2,)),
        ],
        compiler_params=pltpu.CompilerParams(
            collective_id=0, has_side_effects=True, vmem_limit_bytes=48 * 2**20
        ),
        name="exchange",
    )(
        send_index, arrival, blend,
        pool_keys, pool_values, fresh, queries, q_cos, q_sin, t_cos, t_sin,
    )

    z, y, core, half = place(me)
    slots = jnp.arange(4, dtype=jnp.int32)
    slot_passages = ((half + slots // 2) % 2) * 8 + 2 * slots + core
    starts = lookup(recompute_blocks.reshape(-1), slot_passages * RB + z // 2) * BLOCK

    attended = pl.pallas_call(
        attend_kernel,
        out_shape=jax.ShapeDtypeStruct((BLOCK, HEADS * HD), bf16),
        in_specs=[smem, hbm, hbm, vmem],
        out_specs=vmem,
        scratch_shapes=[
            pltpu.VMEM((4, 2, TOK_DEV, WIDTH), bf16),
            pltpu.VMEM((4, 2, TOK_DEV, WIDTH), bf16),
            pltpu.VMEM((4, HEADS, BLOCK, 2 * HD), jnp.float32),
            pltpu.VMEM((4, HEADS, BLOCK, HD), jnp.float32),
            pltpu.VMEM((4, HEADS, BLOCK, HD), bf16),
            pltpu.VMEM((4, BLOCK, HD), jnp.float32),
            pltpu.VMEM((4, HEADS, BLOCK, HD), bf16),
            pltpu.VMEM((4, BLOCK, HD), jnp.float32),
            dma((2,)),
            dma((2, 4)),
            dma((2, 4)),
            dma((2, 4)),
            dma((2, 4)),
            dma((2, 4)),
            dma((2, 4)),
        ],
        compiler_params=pltpu.CompilerParams(
            collective_id=1, has_side_effects=True, vmem_limit_bytes=56 * 2**20
        ),
        name="attend",
    )(starts, key_cache, value_cache, q_group)
    return (key_cache, value_cache, attended)


def solution(mesh):
    placed = (
        P(("seq", "tp"), None, None),
        P(("seq", "tp"), None, None),
        P(),
        P(),
        P(),
        P(),
        P("seq", None),
        P(None, "tp"),
        P(None, "tp"),
        P("seq", "tp"),
    )
    return jax.shard_map(
        on_device,
        mesh=mesh,
        in_specs=placed,
        out_specs=(P("seq", "tp"), P("seq", "tp"), P("seq", "tp")),
        check_vma=False,
    )
```

time: 730 us -> 250 us (0.34)
  Pallas kernels: 0 us -> 224 us
  matrix products: 220 us -> 3.81 us
  waiting for transfers between devices: 163 us -> 0 us
  other arithmetic: 131 us -> 7.54 us
  local copies, waits for them, and re-layouts: 126 us -> 10.5 us
  loops' own time: 45.2 us -> 0 us
  starting transfers between devices: 24.6 us -> 0 us
  between operations: 14.2 us -> 0.95 us
    pallas_call x0 -> x2, Pallas kernels: none -> 224 us  [the longest x1 163 us: on_device(): pl.pallas_call(attend_kernel, out_shape=jax.ShapeDtypeStruct((BLOCK, HEAD...]
    dot_general x64 -> x0, matrix products: 214 us -> none  [the longest x32 118 us: attend_block(): jnp.einsum('hqk,khd->hqd', weights.astype(jnp.bfloat16), value_heads, pre...]
    all_gather x4 -> x0, waiting for transfers between devices: 119 us -> none  [the longest x1 67 us: on_device(): lax.all_gather(key_cache, 'seq', axis=0, tiled=True)]
    reduce_sum x33 -> x0, other arithmetic: 72.3 us -> none  [the longest x32 72.3 us: attend_block(): weight_sum = weight_sum * rescale + jnp.sum(weights, axis=2)]
    dynamic_slice x65 -> x1, local copies, waits for them, and re-layouts: 61.5 us -> 1 us  [on_device(): lax.dynamic_index_in_dim(recompute_blocks, passage, 0, keepdims=False)]
    another operation x33 -> x0, loops' own time: 45.2 us -> none  [the longest x1 43 us: fold_with(): lax.scan(visit_keys, carry_in, (key_blocks, value_blocks, starts))]
    all_to_all x4 -> x0, waiting for transfers between devices: 43.4 us -> none  [the longest x1 14.2 us: on_device(): lax.all_to_all(outgoing(row_keys), 'seq', split_axis=0, concat_axis=0, ti...]
    unnamed x24 -> x20, local copies, waits for them, and re-layouts: 47.8 us -> 7.29 us
  transfers between devices with their start and end apart: 8 -> 0, of which waited for: 6 -> 0; matrix products, arithmetic and copies ran while one was open for 7% -> 0% of each run, Pallas kernels for 0% -> 0%
where the time goes in v1:
time: 250 us; the launch traced here: 247 us
  Pallas kernels  224 us (90%)
  local copies, waits for them, and re-layouts  10.5 us (4%)
  other arithmetic  7.54 us (3%)
  matrix products  3.81 us (2%)
    pallas_call x1, Pallas kernels, on_device(): pl.pallas_call(attend_kernel, out_shape=jax.ShapeDtypeStruct((BLOCK, HEAD...  163 us
    pallas_call x1, Pallas kernels, on_device(): pl.pallas_call(exchange_kernel, out_shape=[jax.ShapeDtypeStruct((TOK_DEV,...  60.3 us
    unnamed x20, local copies, waits for them, and re-layouts  7.29 us

profile of v1, /device:TPU:121, one launch (start us, length us, event | category | flops | bytes accessed | tf_op | source)
XLA Modules:
  0.0 246.6 jit_solution(13967561953673563907)
XLA Ops:
  0.7 1.0 dynamic-slice_reduce_fusion
  1.7 0.1 fusion.28
  1.8 0.7 compare_and_fusion
  2.5 0.7 compare_select_fusion
  3.3 0.7 select_reduce_fusion.3
  4.1 0.1 broadcast_in_dim.113
  4.2 1.3 gather_fusion
  5.5 0.7 select_reduce_fusion
  6.4 0.8 copy.16
  7.1 0.1 broadcast_in_dim.121
  7.2 0.2 select_reduce_fusion.4
  7.4 0.1 select_reduce_fusion.2
  7.5 0.5 broadcast_multiply_fusion.starts
  8.0 0.1 add_select_fusion
  8.1 0.1 broadcast_compare_fusion
  8.2 0.9 convert_reduce_fusion
  9.1 0.1 select_reduce_fusion.1
  9.3 0.1 copy.15
  9.4 0.1 reshape.310.send_index
  9.5 3.1 %fusion = bf16[1,128,256]{2,1,0:T(8,128)(2,1)S(1)} fusion(bf16[128,8192]{1,0:T(8,128)(2,1)S(1)} %copy-done, bf16[8192,256]{1,0:T(8,128)(2,1)} %param.18), kind=kOutput, calls=%fused_computation.2 | convolution fusion | flops 536903680 | bytes 6356992 | tf_op jit(solution)/shard_map/dot_general | solution.py:546
  12.6 0.4 copy-done.7
  13.0 0.8 fusion.30
  13.8 0.2 fusion.29
  14.0 2.1 multiply_cosine_fusion
  16.2 0.2 maximum_multiply_fusion
  16.6 60.3 %exchange.1 = (bf16[1024,256]{1,0:T(8,128)(2,1)S(1)}, bf16[1024,256]{1,0:T(8,128)(2,1)S(1)}, bf16[4,16,128,128]{3,2,1,0:T(8,128)(2,1)}) custom-call(s32[128]{0:T(128)S(1)} %reshape.310.send_index, s32[64]{0:T(128)S(1)} %fusion.27.arrival, s32[2,8]{1,0:T(2,128)S(1)} %add_convert_fusion.1.blend, bf16[32,16,1024]{2,1,0:T(8,128)(2,1)S(1)} %copy-done.4, ...), custom_call_target="tpu_custom_call" | custom-call | tf_op jit(solution)/shard_map/exchange/pallas_call | solution.py:556
  77.0 0.8 copy-done.1
  77.7 0.8 copy-done.3
  78.5 163.5 %attend.1 = bf16[128,2048]{1,0:T(8,128)(2,1)} custom-call(s32[4]{0:T(128)} %broadcast_multiply_fusion.starts, bf16[1024,256]{1,0:T(8,128)(2,1)} %copy-done.3, bf16[1024,256]{1,0:T(8,128)(2,1)} %copy-done.1, bf16[4,16,128,128]{3,2,1,0:T(8,128)(2,1)} %get-tuple-element.8.q_ref), custom_call_target="tpu_custom_call" | custom-call | tf_op jit(solution)/shard_map/attend/pallas_call | solution.py:597
  242.0 1.9 copy.28
  243.9 0.8 copy.29
  244.7 1.9 copy.30
  (37 shorter events, 0.7 us)
Async XLA Ops:
  0.6 8.9 %copy-start = (bf16[128,8192]{1,0:T(8,128)(2,1)S(1)}, bf16[128,8192]{1,0:T(8,128)(2,1)}, u32[]{:S(2)}) copy-start(bf16[128,8192]{1,0:T(8,128)(2,1)} %param.16) | copy-start | bytes 6291460
  9.5 3.5 %copy-start.7 = (bf16[8192,256]{1,0:T(8,128)(2,1)S(1)}, bf16[8192,256]{1,0:T(8,128)(2,1)}, u32[]{:S(2)}) copy-start(bf16[8192,256]{1,0:T(8,128)(2,1)} %param.17) | copy-start | bytes 12582916
  13.7 2.9 %copy-start.4 = (bf16[32,16,1024]{2,1,0:T(8,128)(2,1)S(1)}, bf16[32,16,1024]{2,1,0:T(8,128)(2,1)}, u32[]{:S(2)}) copy-start(bf16[32,16,1024]{2,1,0:T(8,128)(2,1)} %pool_k.1) | copy-start | bytes 3145732
  13.8 2.8 %copy-start.5 = (bf16[32,16,1024]{2,1,0:T(8,128)(2,1)S(1)}, bf16[32,16,1024]{2,1,0:T(8,128)(2,1)}, u32[]{:S(2)}) copy-start(bf16[32,16,1024]{2,1,0:T(8,128)(2,1)} %pool_v.1) | copy-start | bytes 3145732
  13.8 2.8 %copy-start.6 = (bf16[128,2048]{1,0:T(8,128)(2,1)S(1)}, bf16[128,2048]{1,0:T(8,128)(2,1)}, u32[]{:S(2)}) copy-start(bf16[128,2048]{1,0:T(8,128)(2,1)} %queries.1) | copy-start | bytes 1572868
  76.9 0.8 copy-start.1
  77.7 0.8 copy-start.3
  78.5 165.4 %copy-start.2 = (bf16[1024,256]{1,0:T(8,128)(2,1)S(1)}, bf16[1024,256]{1,0:T(8,128)(2,1)}, u32[]{:S(2)}) copy-start(bf16[1024,256]{1,0:T(8,128)(2,1)} %copy-done.1) | copy-start | bytes 1572868

commit v2 on v1

--- a/solution.py
+++ b/solution.py
@@ -39,32 +39,6 @@
     )
 
 
-def tables_at(places):
-    rates = frequencies()
-    angles = places.astype(jnp.float32)[:, None] * jnp.concatenate([rates, rates])[None, :]
-    sign = jnp.where(jnp.arange(HD) < HD // 2, -1.0, 1.0).astype(jnp.float32)
-    return jnp.cos(angles), jnp.sin(angles) * sign[None, :]
-
-
-def lookup(small_table, wanted):
-    matches = wanted[:, None] == jnp.arange(small_table.shape[0], dtype=jnp.int32)[None, :]
-    return jnp.sum(jnp.where(matches, small_table[None, :], 0), axis=1)
-
-
-def row_places(row_ids, recompute_blocks, offsets):
-    passage = row_ids // BLOCK % PASSAGES
-    which_block = row_ids // (PASSAGES * BLOCK)
-    block_start = (
-        lookup(recompute_blocks.reshape(-1), passage * RB + which_block) * BLOCK + row_ids % BLOCK
-    )
-    return lookup(offsets, passage) + block_start
-
-
-def token_positions(first_token, offsets):
-    token_seq = first_token + jnp.arange(TOK_DEV, dtype=jnp.int32)
-    return lookup(offsets, token_seq // PASSAGE_LEN) + token_seq % PASSAGE_LEN
-
-
 def turn(values, cosine, sine):
     return values * cosine + pltpu.roll(values, HD // 2, 1) * sine
 
@@ -85,12 +59,29 @@
     return z, (me // 2) % 4, me % 2, z % 2
 
 
+def group_of(half, core):
+    return lax.rem(half + core, 2)
+
+
+def slot_half(group, slot):
+    return lax.rem(group + slot, 2)
+
+
+def rotation(first, count, rates):
+    places = lax.broadcasted_iota(jnp.int32, (count, HD), 0) + first
+    angles = places.astype(jnp.float32) * rates
+    sine = jnp.sin(angles)
+    lane = lax.broadcasted_iota(jnp.int32, (count, HD), 1)
+    return jnp.cos(angles), jnp.where(lane < HD // 2, -sine, sine)
+
+
 def exchange_kernel(
-    send_index, arrival, blend,
-    pool_k, pool_v, fresh, queries, q_cos, q_sin, t_cos, t_sin,
+    passage_ids, page_slot, offsets, recompute_blocks, rates,
+    pool_k, pool_v, hidden, w_key, w_value, queries,
     out_k, out_v, out_q,
-    rows_k, rows_v, outgoing, arriving_k, arriving_v, turned, fresh_in,
-    own_sem, tp_send, tp_recv, page_send, page_recv, q_send, q_recv, f_send, f_recv,
+    rows_k, rows_v, outgoing, arriving_k, arriving_v, turned, fresh, fresh_in,
+    hidden_buf, w_buf, t_cos, t_sin, used, send_tab, arrival_tab, send_index, arrival,
+    own_sem, load_sem, tp_send, tp_recv, page_send, page_recv, q_send, q_recv, f_send, f_recv,
 ):
     me = lax.axis_index("seq")
     my_tp = lax.axis_index("tp")
@@ -138,12 +129,21 @@
             tp_copy(which, step).start()
         own_copy(which).start()
 
+    loads = [
+        pltpu.make_async_copy(hidden, hidden_buf, load_sem.at[0]),
+        pltpu.make_async_copy(w_key, w_buf.at[0], load_sem.at[1]),
+        pltpu.make_async_copy(w_value, w_buf.at[1], load_sem.at[2]),
+    ]
+    for load in loads:
+        load.start()
+
+    my_passage = lax.rem(me, PASSAGES)
+    my_start = recompute_blocks[my_passage, me // PASSAGES] * BLOCK
+    q_cos, q_sin = rotation(offsets[my_passage] + my_start, BLOCK, rates[...])
     for head in range(HEADS):
         cols = slice(head * HD, (head + 1) * HD)
-        turned[head] = turn(
-            queries[:, cols].astype(jnp.float32), q_cos[...], q_sin[...]
-        ).astype(jnp.bfloat16)
-    group_z = z - half + lax.rem(half + y // 2, 2)
+        turned[head] = turn(queries[:, cols].astype(jnp.float32), q_cos, q_sin).astype(jnp.bfloat16)
+    group_z = z - half + lax.rem(half + y + core, 2)
 
     def q_dest(other_y):
         return group_z * 8 + other_y * 2 + core
@@ -167,7 +167,67 @@
     def f_local():
         return pltpu.make_async_copy(fresh, fresh_in.at[which_block], f_recv.at[which_block])
 
+    for other_y in range(4):
+
+        @pl.when(q_dest(other_y) != me)
+        def _():
+            q_remote(other_y).start()
+
+        @pl.when(q_dest(other_y) == me)
+        def _():
+            q_local().start()
+
+    for row in range(PASSAGES):
+        used[row : row + 1, :] = page_slot[pl.ds(passage_ids[row], 1), :]
+    slots = used[...]
+    lane = lax.broadcasted_iota(jnp.int32, slots.shape, 1)
+    in_half = lax.rem(lane, PER_DEST)
+    hit = (slots >> 7) == me
+    rank = hit.astype(jnp.int32)
+    for shift in (1, 2, 4, 8, 16, 32):
+        rank = rank + jnp.where(in_half >= shift, pltpu.roll(rank, shift, 1), 0)
+    table = jnp.zeros(slots.shape, jnp.int32)
     for side in range(2):
+        for order in range(CAP):
+            wanted = hit & (rank == order + 1) & ((lane >= PER_DEST) == (side == 1))
+            local = jnp.where(wanted, slots & 127, 0)
+            for shift in (64, 32, 16, 8, 4, 2, 1):
+                local = local + pltpu.roll(local, shift, 1)
+            table = jnp.where(lane == side * CAP + order, local, table)
+    send_tab[...] = table
+    source = jnp.broadcast_to(used[pl.ds(me // 2, 1), :], (8, HD)) >> 7
+    lane = lax.broadcasted_iota(jnp.int32, source.shape, 1)
+    in_half = lax.rem(lane, PER_DEST)
+    rank = jnp.zeros(source.shape, jnp.int32)
+    for shift in range(1, PER_DEST):
+        same = (pltpu.roll(source, shift, 1) == source) & (in_half >= shift)
+        rank = rank + same.astype(jnp.int32)
+    arrival_tab[...] = source * CAP + rank
+    index_copies = [
+        pltpu.make_async_copy(send_tab, send_index, load_sem.at[3]),
+        pltpu.make_async_copy(arrival_tab, arrival, load_sem.at[4]),
+    ]
+    for copy in index_copies:
+        copy.start()
+
+    for load in loads:
+        load.wait()
+
+    def multiply(part, totals):
+        depth = pl.ds(pl.multiple_of(part * 1024, 1024), 1024)
+        return tuple(
+            total
+            + jnp.dot(hidden_buf[:, depth], w_buf[which, depth, :], preferred_element_type=jnp.float32)
+            for which, total in enumerate(totals)
+        )
+
+    nothing = jnp.zeros((BLOCK, WIDTH), jnp.float32)
+    raw_k, raw_v = lax.fori_loop(0, 8, multiply, (nothing, nothing))
+    for head in range(2):
+        cols = slice(head * HD, (head + 1) * HD)
+        fresh[0, :, cols] = turn(raw_k[:, cols], q_cos, q_sin).astype(jnp.bfloat16)
+    fresh[1] = raw_v.astype(jnp.bfloat16)
+    for side in range(2):
 
         @pl.when(home + side != me)
         def _():
@@ -177,15 +237,11 @@
         def _():
             f_local().start()
 
-    for other_y in range(4):
-
-        @pl.when(q_dest(other_y) != me)
-        def _():
-            q_remote(other_y).start()
-
-        @pl.when(q_dest(other_y) == me)
-        def _():
-            q_local().start()
+    token_cos, token_sin = rotation(offsets[me // 2] + core * TOK_DEV, TOK_DEV, rates[...])
+    t_cos[...] = token_cos
+    t_sin[...] = token_sin
+    for copy in index_copies:
+        copy.wait()
 
     def page_copy(which, step):
         peer = lax.rem(me + step, N_SEQ)
@@ -213,7 +269,9 @@
         def pick(step, _):
             peer = lax.rem(me + step, N_SEQ)
             for rank in range(CAP):
-                outgoing[which, peer, rank] = rows[which][send_index[peer * CAP + rank]]
+                outgoing[which, peer, rank] = rows[which][
+                    send_index[peer // 2, lax.rem(peer, 2) * CAP + rank]
+                ]
 
             @pl.when(step > 0)
             def _():
@@ -245,8 +303,9 @@
         lax.fori_loop(1, N_SEQ, landed, 0)
 
         def put(page, _):
-            slot = arrival[page]
-            block = page // 8
+            slot = arrival[0, core * PER_DEST + page]
+            block = core * 8 + page // 8
+            first, second = (recompute_blocks[me // 2, number] for number in range(RB))
             where = pl.ds(pl.multiple_of(page * PAGE, PAGE), PAGE)
             within = pl.ds(pl.multiple_of(lax.rem(page, 8) * PAGE, PAGE), PAGE)
             got = arriving[which][slot // CAP, lax.rem(slot, CAP)]
@@ -260,8 +319,9 @@
                     ],
                     axis=1,
                 )
-            new = fresh_in[blend[1, block], which, within]
-            flag = jnp.full(got.shape, blend[0, block], jnp.int32) > 0
+            new = fresh_in[jnp.where(second == block, 1, 0), which, within]
+            here = jnp.full(got.shape, block, jnp.int32)
+            flag = (here == first) | (here == second)
             mixed = jnp.where(flag, new.astype(jnp.float32), got.astype(jnp.float32))
             (out_k, out_v)[which][where] = mixed.astype(jnp.bfloat16)
             return 0
@@ -291,7 +351,7 @@
 
 
 def attend_kernel(
-    starts,
+    recompute_blocks,
     own_k, own_v, q_ref,
     out_ref,
     k_buf, v_buf, acc, peak, part, stat, part_in, stat_in,
@@ -300,6 +360,7 @@
     me = lax.axis_index("seq")
     z, y, core, half = place(me)
     pair = z - half
+    group = group_of(half, core)
     sibling = me + 1 - 2 * core
     barrier = pltpu.get_barrier_semaphore()
 
@@ -337,37 +398,43 @@
             kv_recv.at[which, step], at(level),
         )
 
-    def side_copy(which, step):
-        level = near(4 - step) if step else z
-        source = bufs[which].at[level, core] if step else owns[which]
+    def side_copy(which, step, passed_on):
+        level = near(4 - step)
+        source = bufs[which].at[level, core] if passed_on else owns[which]
         return on_seq(
             source, bufs[which].at[level, core], side_send.at[which, step],
             side_recv.at[which, step], sibling,
         )
 
     def side_landed(which, step):
-        level = near(4 - step) if step else z
+        level = near(4 - step)
         return on_seq(
             owns[which], bufs[which].at[level, 1 - core], side_send.at[which, step],
             side_recv.at[which, step], sibling,
         )
 
+    def pass_on(which):
+        level, ahead = (near(3), near(1)) if which == 0 else (near(1), near(3))
+        return on_seq(
+            bufs[which].at[level, core], bufs[which].at[level, core], kv_send.at[which, 2],
+            kv_recv.at[which, 2], at(ahead),
+        )
+
     for which in range(2):
-        side_copy(which, 0).start()
+        side_copy(which, 0, False).start()
         own_copy(which).start()
-    for step in (1, 3, 2):
-        for which in range(2):
-            kv_copy(which, step).start()
+    for which, step in ((0, 1), (1, 3), (1, 1), (0, 3)):
+        kv_copy(which, step).start()
     acc[...] = jnp.zeros_like(acc)
     peak[...] = jnp.full_like(peak, MASKED)
 
     ones = jnp.ones((PASSAGE_LEN, HD), jnp.bfloat16)
 
     def fold(slot, level, limit):
-        def unit(index, _):
-            for group in range(2):
-                cols = slice(group * HD, (group + 1) * HD)
-                heads = pl.ds(group * 8 + index * UNIT, UNIT)
+        for index in range(8 // UNIT):
+            for kv in range(2):
+                cols = slice(kv * HD, (kv + 1) * HD)
+                heads = slice(kv * 8 + index * UNIT, kv * 8 + (index + 1) * UNIT)
                 q = q_ref[slot, heads].reshape(QT, HD)
                 keys = k_buf[level].reshape(PASSAGE_LEN, WIDTH)[:, cols]
                 values = v_buf[level].reshape(PASSAGE_LEN, WIDTH)[:, cols]
@@ -389,12 +456,9 @@
                 before = acc[slot, heads].reshape(QT, 2 * HD)
                 acc[slot, heads] = (before * keep[:, :1] + total).reshape(UNIT, BLOCK, 2 * HD)
                 peak[slot, heads] = new.reshape(UNIT, BLOCK, HD)
-            return 0
-
-        lax.fori_loop(0, 8 // UNIT, unit, 0)
 
     def slot_passage(slot):
-        return lax.rem(half + slot // 2, 2) * 8 + 2 * slot + core
+        return slot_half(group, slot) * 8 + 2 * slot + core
 
     def visit(slot, level):
         passage = level * 4 + y
@@ -406,10 +470,10 @@
 
         @pl.when(passage == mine)
         def _():
-            fold(slot, level, starts[slot])
+            fold(slot, level, recompute_blocks[mine, z // 2] * BLOCK)
 
     def owner(slot):
-        return (pair + lax.rem(half + slot // 2, 2)) * 8 + slot * 2 + core
+        return (pair + slot_half(group, slot)) * 8 + slot * 2 + core
 
     def part_copies(slot):
         return (
@@ -451,24 +515,56 @@
             for copy in local_copies(slot):
                 copy.start()
 
-    for step in (0, 1, 3, 2):
-        level = near(4 - step) if step else z
-        for which in range(2):
-            if step:
-                kv_landed(which, step).wait_recv()
-                side_copy(which, step).start()
-            else:
+    def ranked(order):
+        return 2 * lax.rem(order, 2) + lax.rem(order // 2 + group, 2)
+
+    def arrive(turn_index, _):
+        @pl.when(turn_index == 0)
+        def _():
+            for which in range(2):
                 own_copy(which).wait()
-        for which in range(2):
-            side_landed(which, step).wait_recv()
-
-        def each(slot, _):
-            visit(slot, level)
-            if step == 2:
+                side_landed(which, 0).wait_recv()
+
+        @pl.when(turn_index == 1)
+        def _():
+            kv_landed(1, 1).wait_recv()
+            side_copy(1, 1, True).start()
+            kv_landed(0, 3).wait_recv()
+            side_copy(0, 3, True).start()
+            for which in range(2):
+                side_landed(which, 1).wait_recv()
+
+        @pl.when(turn_index == 2)
+        def _():
+            for which in range(2):
+                kv_landed(which, 2).wait_recv()
+                side_copy(which, 2, True).start()
+                side_landed(which, 3).wait_recv()
+            for which in range(2):
+                side_landed(which, 2).wait_recv()
+
+        def each(order, _):
+            slot = ranked(jnp.where(turn_index == 2, order // 2, 3 - order))
+            step = jnp.where(turn_index == 2, 3 - lax.rem(order, 2), turn_index)
+            visit(slot, near(4 - step))
+
+            @pl.when((turn_index == 0) & (order == 1))
+            def _():
+                for which, early_step in ((0, 1), (1, 3)):
+                    kv_landed(which, early_step).wait_recv()
+                    pass_on(which).start()
+                    side_copy(which, early_step, True).start()
+
+            @pl.when((turn_index == 2) & (lax.rem(order, 2) == 1))
+            def _():
                 give_back(slot)
+
             return 0
 
-        lax.fori_loop(0, 4, each, 0)
+        lax.fori_loop(0, jnp.where(turn_index == 2, 8, 4), each, 0)
+        return 0
+
+    lax.fori_loop(0, 3, arrive, 0)
 
     for slot in range(4):
         on_seq(part.at[0], part_in.at[slot], part_send.at[0, 0], part_recv.at[0, slot],
@@ -488,10 +584,11 @@
         out_ref[:, head * HD : (head + 1) * HD] = result.astype(jnp.bfloat16)
 
     for which in range(2):
-        for step in (1, 3, 2):
+        for step in (1, 3):
             kv_copy(which, step).wait_send()
+        pass_on(which).wait_send()
         for step in range(4):
-            side_copy(which, step).wait_send()
+            side_copy(which, step, step > 0).wait_send()
     for slot in range(4):
 
         @pl.when(owner(slot) != me)
@@ -512,42 +609,8 @@
     w_value,
     queries,
 ):
-    me = lax.axis_index("seq")
-    row_pages = N_TP * pool_keys.shape[0]
-    used_slots = jnp.take(page_slot, passage_ids, axis=0).reshape(N_SEQ, PER_DEST)
-    source_row = used_slots // row_pages
-    row_local = used_slots % row_pages
-    position_ids = jnp.arange(PER_DEST, dtype=jnp.int32)
-    earlier = position_ids[None, :] < position_ids[:, None]
-    same_source = source_row[:, :, None] == source_row[:, None, :]
-    page_rank = jnp.sum(same_source & earlier[None, :, :], axis=2)
-    slot_hit = (source_row == me)[:, :, None] & (
-        page_rank[:, :, None] == jnp.arange(CAP, dtype=jnp.int32)[None, None, :]
-    )
-    send_index = jnp.sum(jnp.where(slot_hit, row_local[:, :, None], 0), axis=1).reshape(-1)
-    my_source = lax.dynamic_index_in_dim(source_row, me, 0, keepdims=False)
-    my_rank = lax.dynamic_index_in_dim(page_rank, me, 0, keepdims=False)
-    arrival = my_source * CAP + my_rank
-
-    passage = me // 2
-    blocks = lax.dynamic_index_in_dim(recompute_blocks, passage, 0, keepdims=False)
-    here = (me % 2) * 8 + jnp.arange(8, dtype=jnp.int32)
-    hit = blocks[:, None] == here[None, :]
-    blend = jnp.stack([jnp.any(hit, axis=0).astype(jnp.int32), hit[1].astype(jnp.int32)])
-
-    row_pos = row_places(me * BLOCK + jnp.arange(BLOCK, dtype=jnp.int32), recompute_blocks, offsets)
-    token_pos = token_positions(me * TOK_DEV, offsets)
-    cosine, sine = tables_at(jnp.concatenate([row_pos, token_pos]))
-    q_cos, t_cos = cosine[:BLOCK], cosine[BLOCK:]
-    q_sin, t_sin = sine[:BLOCK], sine[BLOCK:]
-    raw = jnp.dot(hidden_rows, w_key, preferred_element_type=jnp.float32).reshape(BLOCK, 2, HD)
-    swapped = jnp.concatenate([raw[..., HD // 2 :], raw[..., : HD // 2]], axis=-1)
-    fresh_keys = (raw * q_cos[:, None, :] + swapped * q_sin[:, None, :]).astype(jnp.bfloat16)
-    fresh_values = jnp.dot(hidden_rows, w_value, preferred_element_type=jnp.float32).astype(
-        jnp.bfloat16
-    )
-    fresh = jnp.stack([fresh_keys.reshape(BLOCK, WIDTH), fresh_values])
-
+    rates = frequencies()
+    rates = jnp.concatenate([rates, rates])[None, :]
     vmem = pl.BlockSpec(memory_space=pltpu.VMEM)
     smem = pl.BlockSpec(memory_space=pltpu.SMEM)
     hbm = pl.BlockSpec(memory_space=pl.ANY)
@@ -560,7 +623,7 @@
             jax.ShapeDtypeStruct((TOK_DEV, WIDTH), bf16),
             jax.ShapeDtypeStruct((4, HEADS, BLOCK, HD), bf16),
         ],
-        in_specs=[smem, smem, smem, hbm, hbm, vmem, vmem, vmem, vmem, vmem, vmem],
+        in_specs=[smem, vmem, smem, smem, vmem, hbm, hbm, hbm, hbm, hbm, vmem],
         out_specs=[vmem, vmem, hbm],
         scratch_shapes=[
             pltpu.VMEM((128, PAGE, WIDTH), bf16),
@@ -569,8 +632,19 @@
             pltpu.VMEM((N_SEQ, CAP, PAGE, WIDTH), bf16),
             pltpu.VMEM((N_SEQ, CAP, PAGE, WIDTH), bf16),
             pltpu.VMEM((HEADS, BLOCK, HD), bf16),
+            pltpu.VMEM((2, BLOCK, WIDTH), bf16),
             pltpu.VMEM((RB, 2, BLOCK, WIDTH), bf16),
+            pltpu.VMEM((BLOCK, 8192), bf16),
+            pltpu.VMEM((2, 8192, WIDTH), bf16),
+            pltpu.VMEM((TOK_DEV, HD), jnp.float32),
+            pltpu.VMEM((TOK_DEV, HD), jnp.float32),
+            pltpu.VMEM((PASSAGES, HD), jnp.int32),
+            pltpu.VMEM((PASSAGES, HD), jnp.int32),
+            pltpu.VMEM((8, HD), jnp.int32),
+            pltpu.SMEM((PASSAGES, HD), jnp.int32),
+            pltpu.SMEM((8, HD), jnp.int32),
             dma((2,)),
+            dma((5,)),
             dma((2, N_TP)),
             dma((2, N_TP)),
             dma((2, N_SEQ)),
@@ -585,14 +659,9 @@
         ),
         name="exchange",
     )(
-        send_index, arrival, blend,
-        pool_keys, pool_values, fresh, queries, q_cos, q_sin, t_cos, t_sin,
+        passage_ids, page_slot, offsets, recompute_blocks, rates,
+        pool_keys, pool_values, hidden_rows, w_key, w_value, queries,
     )
-
-    z, y, core, half = place(me)
-    slots = jnp.arange(4, dtype=jnp.int32)
-    slot_passages = ((half + slots // 2) % 2) * 8 + 2 * slots + core
-    starts = lookup(recompute_blocks.reshape(-1), slot_passages * RB + z // 2) * BLOCK
 
     attended = pl.pallas_call(
         attend_kernel,
@@ -620,7 +689,7 @@
             collective_id=1, has_side_effects=True, vmem_limit_bytes=56 * 2**20
         ),
         name="attend",
-    )(starts, key_cache, value_cache, q_group)
+    )(recompute_blocks, key_cache, value_cache, q_group)
     return (key_cache, value_cache, attended)
 
 

time: 250 us -> 181 us (0.72); the launches traced: 247 us -> 180 us
  Pallas kernels: 224 us -> 166 us
  other arithmetic: 7.54 us -> 0.1 us
  matrix products: 3.81 us -> 0 us
  local copies, waits for them, and re-layouts: 10.5 us -> 13.7 us
    pallas_call x1, Pallas kernels: 163 us -> 105 us  [on_device(): pl.pallas_call(attend_kernel, out_shape=jax.ShapeDtypeStruct((BLOCK, HEAD...]
    unnamed x20 -> x26, local copies, waits for them, and re-layouts: 7.29 us -> 13.7 us
    dot_general x2 -> x0, matrix products: 3.81 us -> none  [the longest x1 3.06 us: on_device(): jnp.dot(hidden_rows, w_value, preferred_element_type=jnp.float32)]
    reduce_sum x6 -> x0, other arithmetic: 2.83 us -> none  [the longest x4 1.75 us: lookup(): return jnp.sum(jnp.where(matches, small_table[None, :], 0), axis=1)]
where the time goes in v2:
time: 181 us; the launch traced here: 180 us
  Pallas kernels  166 us (92%)
  local copies, waits for them, and re-layouts  13.7 us (8%)
    pallas_call x1, Pallas kernels, on_device(): pl.pallas_call(attend_kernel, out_shape=jax.ShapeDtypeStruct((BLOCK, HEAD...  105 us
    pallas_call x1, Pallas kernels, on_device(): pl.pallas_call(exchange_kernel, out_shape=[jax.ShapeDtypeStruct((TOK_DEV,...  60.7 us
    unnamed x26, local copies, waits for them, and re-layouts  13.7 us

profile of v2, /device:TPU:121, one launch (start us, length us, event | category | flops | bytes accessed | tf_op | source)
XLA Modules:
  0.0 180.3 jit_solution(1259120544880346785)
XLA Ops:
  0.7 0.1 maximum_bitcast_fusion.rates
  0.7 0.8 copy.13.recompute_blocks
  1.5 0.0 copy-start.4
  1.5 1.2 copy-done.4
  2.7 0.0 copy-start.5
  2.7 1.2 copy-done.5
  3.9 0.0 copy-start.6
  3.9 1.0 copy-done.6
  5.0 0.0 copy-start.8
  5.0 0.7 copy-done.8
  5.7 0.0 copy-start.9
  5.7 0.7 copy-done.9
  6.4 0.0 copy-start.10
  6.4 0.7 copy-done.10
  7.0 0.0 copy-start.7
  7.0 60.7 %exchange.1 = (bf16[1024,256]{1,0:T(8,128)(2,1)S(1)}, bf16[1024,256]{1,0:T(8,128)(2,1)S(1)}, bf16[4,16,128,128]{3,2,1,0:T(8,128)(2,1)S(1)}) custom-call(s32[16]{0:T(128)S(1)} %copy-done.9, s32[32,128]{1,0:T(8,128)S(1)} %copy-done.8, s32[16]{0:T(128)S(1)} %copy-done.10, s32[16,2]{1,0:T(8,128)S(1)} %copy.13.recompute_blocks, ...), custom_call_target="tpu_custom_call" | custom-call | tf_op jit(solution)/shard_map/exchange/pallas_call | solution.py:619
  67.7 0.0 copy-done.7
  67.7 0.0 copy-start
  67.7 1.3 copy-done
  69.0 0.0 copy-start.1
  69.0 0.8 copy-done.1
  69.8 0.0 copy-start.3
  69.8 0.8 copy-done.3
  70.6 0.0 copy-start.2
  70.6 105.1 %attend.1 = bf16[128,2048]{1,0:T(8,128)(2,1)} custom-call(s32[16,2]{1,0:T(8,128)} %copy-done.7, bf16[1024,256]{1,0:T(8,128)(2,1)} %copy-done.3, bf16[1024,256]{1,0:T(8,128)(2,1)} %copy-done.1, bf16[4,16,128,128]{3,2,1,0:T(8,128)(2,1)} %copy-done), custom_call_target="tpu_custom_call" | custom-call | tf_op jit(solution)/shard_map/attend/pallas_call | solution.py:666
  175.8 1.9 %copy.18 = bf16[1024,256]{1,0:T(8,128)(2,1)} copy(bf16[1024,256]{1,0:T(8,128)(2,1)} %copy-done.3) | data formatting | bytes 1048576
  177.6 0.0 copy-done.2
  177.6 0.8 copy.19
  178.4 1.9 %copy.20 = bf16[128,2048]{1,0:T(8,128)(2,1)} copy(bf16[128,2048]{1,0:T(8,128)(2,1)} %attend.1) | data formatting | bytes 1048576
  (1 shorter events, 0.0 us)
Async XLA Ops:
  1.5 1.2 copy-start.4
  2.7 1.2 copy-start.5
  3.9 1.0 copy-start.6
  5.0 0.7 copy-start.8
  5.7 0.7 copy-start.9
  6.4 0.7 copy-start.10
  7.0 60.7 %copy-start.7 = (s32[16,2]{1,0:T(8,128)}, s32[16,2]{1,0:T(8,128)S(1)}, u32[]{:S(2)}) copy-start(s32[16,2]{1,0:T(8,128)S(1)} %copy.13.recompute_blocks) | copy-start | bytes 388
  67.7 1.3 copy-start
  69.0 0.8 copy-start.1
  69.8 0.8 copy-start.3
  70.6 107.0 %copy-start.2 = (bf16[1024,256]{1,0:T(8,128)(2,1)S(1)}, bf16[1024,256]{1,0:T(8,128)(2,1)}, u32[]{:S(2)}) copy-start(bf16[1024,256]{1,0:T(8,128)(2,1)} %copy-done.1) | copy-start | bytes 1572868

commit v3 on v2

--- a/solution.py
+++ b/solution.py
@@ -2,6 +2,7 @@
 
 import jax
 import jax.numpy as jnp
+import numpy as np
 from jax import lax
 from jax.experimental import pallas as pl
 from jax.experimental.pallas import tpu as pltpu
@@ -29,14 +30,14 @@
 
 
 def frequencies():
-    exponent = jnp.arange(0, HD, 2, dtype=jnp.float32) / HD
-    base_rate = jnp.power(jnp.float32(500000.0), -exponent)
+    base_rate = 500000.0 ** (-np.arange(0, HD, 2) / HD)
     wave_length = 2.0 * math.pi / base_rate
     smooth = (8192.0 / wave_length - 1.0) / 3.0
     blended = (1.0 - smooth) * base_rate / 8.0 + smooth * base_rate
-    return jnp.where(
-        wave_length > 8192.0, base_rate / 8.0, jnp.where(wave_length < 2048.0, base_rate, blended)
+    rates = np.where(
+        wave_length > 8192.0, base_rate / 8.0, np.where(wave_length < 2048.0, base_rate, blended)
     )
+    return np.concatenate([rates, rates])[None, :].astype(np.float32)
 
 
 def turn(values, cosine, sine):
@@ -59,12 +60,12 @@
     return z, (me // 2) % 4, me % 2, z % 2
 
 
-def group_of(half, core):
-    return lax.rem(half + core, 2)
-
-
-def slot_half(group, slot):
-    return lax.rem(group + slot, 2)
+def home_level(z, core, slot):
+    return lax.rem(z + lax.rem(core + slot, 2) * (3 - 2 * (slot // 2)), 4)
+
+
+def group_home(z, core, y):
+    return lax.rem(z + lax.rem(core + y, 2) * (1 + 2 * (y // 2)), 4)
 
 
 def rotation(first, count, rates):
@@ -75,13 +76,15 @@
     return jnp.cos(angles), jnp.where(lane < HD // 2, -sine, sine)
 
 
-def exchange_kernel(
+def blend_kernel(
     passage_ids, page_slot, offsets, recompute_blocks, rates,
     pool_k, pool_v, hidden, w_key, w_value, queries,
-    out_k, out_v, out_q,
-    rows_k, rows_v, outgoing, arriving_k, arriving_v, turned, fresh, fresh_in,
+    out_k, out_v, out_ref,
+    query_buf, slot_buf, q_group, rows_k, rows_v, outgoing, arriving_k, arriving_v, turned, fresh, fresh_in,
     hidden_buf, w_buf, t_cos, t_sin, used, send_tab, arrival_tab, send_index, arrival,
+    k_buf, v_buf, acc, peak, part, stat, part_in, stat_in,
     own_sem, load_sem, tp_send, tp_recv, page_send, page_recv, q_send, q_recv, f_send, f_recv,
+    out_sem, kv_send, kv_recv, side_send, side_recv, part_send, part_recv,
 ):
     me = lax.axis_index("seq")
     my_tp = lax.axis_index("tp")
@@ -99,7 +102,76 @@
         pl.semaphore_signal(
             barrier, inc=1, device_id={"tp": lax.rem(my_tp + step, N_TP)}, device_id_type=MESH
         )
+
+    loads = [
+        pltpu.make_async_copy(hidden, hidden_buf, load_sem.at[0]),
+        pltpu.make_async_copy(w_key, w_buf.at[0], load_sem.at[1]),
+        pltpu.make_async_copy(w_value, w_buf.at[1], load_sem.at[2]),
+        pltpu.make_async_copy(queries, query_buf, load_sem.at[5]),
+        pltpu.make_async_copy(page_slot, slot_buf, load_sem.at[6]),
+    ]
+    for load in loads:
+        load.start()
+
+    loads[3].wait()
+    my_passage = lax.rem(me, PASSAGES)
+    my_start = recompute_blocks[my_passage * RB + me // PASSAGES] * BLOCK
+    q_cos, q_sin = rotation(offsets[my_passage] + my_start, BLOCK, rates[...])
+    for head in range(HEADS):
+        cols = slice(head * HD, (head + 1) * HD)
+        turned[head] = turn(query_buf[:, cols].astype(jnp.float32), q_cos, q_sin).astype(jnp.bfloat16)
+    acc[...] = jnp.zeros_like(acc)
+    peak[...] = jnp.full_like(peak, MASKED)
     pl.semaphore_wait(barrier, N_SEQ - 1 + N_TP - 1)
+
+    group = lax.rem(half + core, 2)
+    sibling = me + 1 - 2 * core
+    bufs = (k_buf, v_buf)
+
+    def near(step):
+        return lax.rem(z + step, 4)
+
+    def at(level):
+        return level * 8 + y * 2 + core
+
+    def keep_copy(which):
+        return pltpu.make_async_copy(
+            bufs[which].at[z, core], (out_k, out_v)[which], out_sem.at[which]
+        )
+
+    def kv_copy(which, step):
+        return on_seq(
+            bufs[which].at[z, core], bufs[which].at[z, core], kv_send.at[which, step],
+            kv_recv.at[which, step], at(near(step)),
+        )
+
+    def kv_landed(which, step):
+        level = near(4 - step)
+        return on_seq(
+            bufs[which].at[z, core], bufs[which].at[level, core], kv_send.at[which, step],
+            kv_recv.at[which, step], at(level),
+        )
+
+    def side_copy(which, step):
+        level = near(4 - step)
+        return on_seq(
+            bufs[which].at[level, core], bufs[which].at[level, core], side_send.at[which, step],
+            side_recv.at[which, step], sibling,
+        )
+
+    def side_landed(which, step):
+        level = near(4 - step)
+        return on_seq(
+            bufs[which].at[z, core], bufs[which].at[level, 1 - core], side_send.at[which, step],
+            side_recv.at[which, step], sibling,
+        )
+
+    def pass_on(which):
+        level, ahead = (near(3), near(1)) if which == 0 else (near(1), near(3))
+        return on_seq(
+            bufs[which].at[level, core], bufs[which].at[level, core], kv_send.at[which, 2],
+            kv_recv.at[which, 2], at(ahead),
+        )
 
     pools = (pool_k, pool_v)
     rows = (rows_k, rows_v)
@@ -124,37 +196,25 @@
             columns(which, my_tp), rows[which].at[pl.ds(my_tp * 32, 32)], own_sem.at[which]
         )
 
-    for which in range(2):
+    def tp_start(which):
         for step in (1, 3, 2):
             tp_copy(which, step).start()
         own_copy(which).start()
 
-    loads = [
-        pltpu.make_async_copy(hidden, hidden_buf, load_sem.at[0]),
-        pltpu.make_async_copy(w_key, w_buf.at[0], load_sem.at[1]),
-        pltpu.make_async_copy(w_value, w_buf.at[1], load_sem.at[2]),
-    ]
-    for load in loads:
-        load.start()
-
-    my_passage = lax.rem(me, PASSAGES)
-    my_start = recompute_blocks[my_passage, me // PASSAGES] * BLOCK
-    q_cos, q_sin = rotation(offsets[my_passage] + my_start, BLOCK, rates[...])
-    for head in range(HEADS):
-        cols = slice(head * HD, (head + 1) * HD)
-        turned[head] = turn(queries[:, cols].astype(jnp.float32), q_cos, q_sin).astype(jnp.bfloat16)
-    group_z = z - half + lax.rem(half + y + core, 2)
+    tp_start(0)
+
+    group_z = group_home(z, core, y)
 
     def q_dest(other_y):
         return group_z * 8 + other_y * 2 + core
 
     def q_remote(other_y):
         return on_seq(
-            turned, out_q.at[y], q_send.at[other_y], q_recv.at[y], q_dest(other_y)
+            turned, q_group.at[y], q_send.at[other_y], q_recv.at[y], q_dest(other_y)
         )
 
     def q_local():
-        return pltpu.make_async_copy(turned, out_q.at[y], q_recv.at[y])
+        return pltpu.make_async_copy(turned, q_group.at[y], q_recv.at[y])
 
     which_block = me // PASSAGES
     home = lax.rem(me, PASSAGES) * 2
@@ -177,8 +237,9 @@
         def _():
             q_local().start()
 
+    loads[4].wait()
     for row in range(PASSAGES):
-        used[row : row + 1, :] = page_slot[pl.ds(passage_ids[row], 1), :]
+        used[row : row + 1, :] = slot_buf[pl.ds(passage_ids[row], 1), :]
     slots = used[...]
     lane = lax.broadcasted_iota(jnp.int32, slots.shape, 1)
     in_half = lax.rem(lane, PER_DEST)
@@ -210,7 +271,8 @@
     for copy in index_copies:
         copy.start()
 
-    for load in loads:
+
+    for load in loads[:3]:
         load.wait()
 
     def multiply(part, totals):
@@ -265,6 +327,8 @@
                 device_id_type=MESH,
             ).wait_recv()
         own_copy(which).wait()
+        if which == 0:
+            tp_start(1)
 
         def pick(step, _):
             peer = lax.rem(me + step, N_SEQ)
@@ -283,7 +347,7 @@
         arriving[which][me] = outgoing[which, me]
 
     for slot in range(4):
-        on_seq(turned, out_q.at[slot], q_send.at[0], q_recv.at[slot], me).wait_recv()
+        on_seq(turned, q_group.at[slot], q_send.at[0], q_recv.at[slot], me).wait_recv()
     for slot in range(2):
         on_seq(fresh, fresh_in.at[slot], f_send.at[0], f_recv.at[slot], me).wait_recv()
 
@@ -302,131 +366,31 @@
 
         lax.fori_loop(1, N_SEQ, landed, 0)
 
-        def put(page, _):
-            slot = arrival[0, core * PER_DEST + page]
-            block = core * 8 + page // 8
-            first, second = (recompute_blocks[me // 2, number] for number in range(RB))
-            where = pl.ds(pl.multiple_of(page * PAGE, PAGE), PAGE)
-            within = pl.ds(pl.multiple_of(lax.rem(page, 8) * PAGE, PAGE), PAGE)
-            got = arriving[which][slot // CAP, lax.rem(slot, CAP)]
-            if which == 0:
-                wide = got.astype(jnp.float32)
-                cosine, sine = t_cos[where], t_sin[where]
-                got = jnp.concatenate(
-                    [
-                        turn(wide[:, :HD], cosine, sine).astype(jnp.bfloat16),
-                        turn(wide[:, HD:], cosine, sine).astype(jnp.bfloat16),
-                    ],
-                    axis=1,
-                )
-            new = fresh_in[jnp.where(second == block, 1, 0), which, within]
-            here = jnp.full(got.shape, block, jnp.int32)
+        def put(index, _):
+            block = core * 8 + index
+            first, second = (recompute_blocks[me // 2 * RB + number] for number in range(RB))
+            here = jnp.full((PAGE, WIDTH), block, jnp.int32)
             flag = (here == first) | (here == second)
-            mixed = jnp.where(flag, new.astype(jnp.float32), got.astype(jnp.float32))
-            (out_k, out_v)[which][where] = mixed.astype(jnp.bfloat16)
+            for page in range(8):
+                slot = arrival[0, core * PER_DEST + index * 8 + page]
+                where = pl.ds(pl.multiple_of(index * BLOCK + page * PAGE, PAGE), PAGE)
+                got = arriving[which][slot // CAP, lax.rem(slot, CAP)].astype(jnp.float32)
+                if which == 0:
+                    cosine, sine = t_cos[where], t_sin[where]
+                    got = jnp.concatenate(
+                        [turn(got[:, :HD], cosine, sine), turn(got[:, HD:], cosine, sine)], axis=1
+                    )
+                within = slice(page * PAGE, (page + 1) * PAGE)
+                new = fresh_in[jnp.where(second == block, 1, 0), which, within]
+                mixed = jnp.where(flag, new.astype(jnp.float32), got)
+                bufs[which][z, core, where] = mixed.astype(jnp.bfloat16)
             return 0
 
-        lax.fori_loop(0, PER_DEST, put, 0)
-
-    for which in range(2):
-        for step in range(1, N_TP):
-            tp_copy(which, step).wait_send()
-
-        def sent(step, _):
-            page_copy(which, step).wait_send()
-            return 0
-
-        lax.fori_loop(1, N_SEQ, sent, 0)
-    for other_y in range(4):
-
-        @pl.when(q_dest(other_y) != me)
-        def _():
-            q_remote(other_y).wait_send()
-
-    for side in range(2):
-
-        @pl.when(home + side != me)
-        def _():
-            f_remote(side).wait_send()
-
-
-def attend_kernel(
-    recompute_blocks,
-    own_k, own_v, q_ref,
-    out_ref,
-    k_buf, v_buf, acc, peak, part, stat, part_in, stat_in,
-    own_sem, kv_send, kv_recv, side_send, side_recv, part_send, part_recv,
-):
-    me = lax.axis_index("seq")
-    z, y, core, half = place(me)
-    pair = z - half
-    group = group_of(half, core)
-    sibling = me + 1 - 2 * core
-    barrier = pltpu.get_barrier_semaphore()
-
-    def greet(step, _):
-        pl.semaphore_signal(
-            barrier, inc=1, device_id={"seq": lax.rem(me + step, N_SEQ)}, device_id_type=MESH
-        )
-        return 0
-
-    lax.fori_loop(1, N_SEQ, greet, 0)
-    pl.semaphore_wait(barrier, N_SEQ - 1)
-
-    owns = (own_k, own_v)
-    bufs = (k_buf, v_buf)
-
-    def near(step):
-        return lax.rem(z + step, 4)
-
-    def at(level):
-        return level * 8 + y * 2 + core
-
-    def own_copy(which):
-        return pltpu.make_async_copy(owns[which], bufs[which].at[z, core], own_sem.at[which])
-
-    def kv_copy(which, step):
-        return on_seq(
-            owns[which], bufs[which].at[z, core], kv_send.at[which, step],
-            kv_recv.at[which, step], at(near(step)),
-        )
-
-    def kv_landed(which, step):
-        level = near(4 - step)
-        return on_seq(
-            owns[which], bufs[which].at[level, core], kv_send.at[which, step],
-            kv_recv.at[which, step], at(level),
-        )
-
-    def side_copy(which, step, passed_on):
-        level = near(4 - step)
-        source = bufs[which].at[level, core] if passed_on else owns[which]
-        return on_seq(
-            source, bufs[which].at[level, core], side_send.at[which, step],
-            side_recv.at[which, step], sibling,
-        )
-
-    def side_landed(which, step):
-        level = near(4 - step)
-        return on_seq(
-            owns[which], bufs[which].at[level, 1 - core], side_send.at[which, step],
-            side_recv.at[which, step], sibling,
-        )
-
-    def pass_on(which):
-        level, ahead = (near(3), near(1)) if which == 0 else (near(1), near(3))
-        return on_seq(
-            bufs[which].at[level, core], bufs[which].at[level, core], kv_send.at[which, 2],
-            kv_recv.at[which, 2], at(ahead),
-        )
-
-    for which in range(2):
-        side_copy(which, 0, False).start()
-        own_copy(which).start()
-    for which, step in ((0, 1), (1, 3), (1, 1), (0, 3)):
-        kv_copy(which, step).start()
-    acc[...] = jnp.zeros_like(acc)
-    peak[...] = jnp.full_like(peak, MASKED)
+        lax.fori_loop(0, 8, put, 0)
+        keep_copy(which).start()
+        side_copy(which, 0).start()
+        for step in (1, 3):
+            kv_copy(which, step).start()
 
     ones = jnp.ones((PASSAGE_LEN, HD), jnp.bfloat16)
 
@@ -435,7 +399,7 @@
             for kv in range(2):
                 cols = slice(kv * HD, (kv + 1) * HD)
                 heads = slice(kv * 8 + index * UNIT, kv * 8 + (index + 1) * UNIT)
-                q = q_ref[slot, heads].reshape(QT, HD)
+                q = q_group[slot, heads].reshape(QT, HD)
                 keys = k_buf[level].reshape(PASSAGE_LEN, WIDTH)[:, cols]
                 values = v_buf[level].reshape(PASSAGE_LEN, WIDTH)[:, cols]
                 score = lax.dot_general(q, keys, BY_KEY, preferred_element_type=jnp.float32)
@@ -458,7 +422,7 @@
                 peak[slot, heads] = new.reshape(UNIT, BLOCK, HD)
 
     def slot_passage(slot):
-        return slot_half(group, slot) * 8 + 2 * slot + core
+        return lax.rem(group + slot, 2) * 8 + 2 * slot + core
 
     def visit(slot, level):
         passage = level * 4 + y
@@ -470,10 +434,10 @@
 
         @pl.when(passage == mine)
         def _():
-            fold(slot, level, recompute_blocks[mine, z // 2] * BLOCK)
+            fold(slot, level, recompute_blocks[mine * RB + home_level(z, core, slot) // 2] * BLOCK)
 
     def owner(slot):
-        return (pair + slot_half(group, slot)) * 8 + slot * 2 + core
+        return home_level(z, core, slot) * 8 + slot * 2 + core
 
     def part_copies(slot):
         return (
@@ -502,7 +466,7 @@
             return jnp.where(lane == head, size, logs)
 
         stat[slot] = lax.fori_loop(
-            0, HEADS, head_part, jnp.full((BLOCK, HD), MASKED, jnp.float32)
+            0, HEADS, head_part, jnp.full((BLOCK, HD), MASKED, jnp.float32), unroll=4
         )
 
         @pl.when(owner(slot) != me)
@@ -522,49 +486,64 @@
         @pl.when(turn_index == 0)
         def _():
             for which in range(2):
-                own_copy(which).wait()
                 side_landed(which, 0).wait_recv()
 
         @pl.when(turn_index == 1)
         def _():
             kv_landed(1, 1).wait_recv()
-            side_copy(1, 1, True).start()
+            side_copy(1, 1).start()
             kv_landed(0, 3).wait_recv()
-            side_copy(0, 3, True).start()
+            side_copy(0, 3).start()
             for which in range(2):
                 side_landed(which, 1).wait_recv()
 
         @pl.when(turn_index == 2)
         def _():
             for which in range(2):
+                side_landed(which, 3).wait_recv()
+
+        step = jnp.where(turn_index < 2, turn_index, 5 - turn_index)
+        level = near(4 - step)
+
+        @pl.when(turn_index == 3)
+        def _():
+            def early(order, _):
+                slot = ranked(order)
+
+                @pl.when(slot_passage(slot) < level * 4 + y)
+                def _():
+                    give_back(slot)
+
+                return 0
+
+            lax.fori_loop(0, 4, early, 0)
+            for which in range(2):
                 kv_landed(which, 2).wait_recv()
-                side_copy(which, 2, True).start()
-                side_landed(which, 3).wait_recv()
+                side_copy(which, 2).start()
             for which in range(2):
                 side_landed(which, 2).wait_recv()
 
         def each(order, _):
-            slot = ranked(jnp.where(turn_index == 2, order // 2, 3 - order))
-            step = jnp.where(turn_index == 2, 3 - lax.rem(order, 2), turn_index)
-            visit(slot, near(4 - step))
+            slot = ranked(jnp.where(turn_index == 3, order, 3 - order))
+            visit(slot, level)
 
             @pl.when((turn_index == 0) & (order == 1))
             def _():
                 for which, early_step in ((0, 1), (1, 3)):
                     kv_landed(which, early_step).wait_recv()
                     pass_on(which).start()
-                    side_copy(which, early_step, True).start()
-
-            @pl.when((turn_index == 2) & (lax.rem(order, 2) == 1))
+                    side_copy(which, early_step).start()
+
+            @pl.when((turn_index == 3) & (slot_passage(slot) >= level * 4 + y))
             def _():
                 give_back(slot)
 
             return 0
 
-        lax.fori_loop(0, jnp.where(turn_index == 2, 8, 4), each, 0)
+        lax.fori_loop(0, 4, each, 0)
         return 0
 
-    lax.fori_loop(0, 3, arrive, 0)
+    lax.fori_loop(0, 4, arrive, 0)
 
     for slot in range(4):
         on_seq(part.at[0], part_in.at[slot], part_send.at[0, 0], part_recv.at[0, slot],
@@ -588,13 +567,41 @@
             kv_copy(which, step).wait_send()
         pass_on(which).wait_send()
         for step in range(4):
-            side_copy(which, step, step > 0).wait_send()
+            side_copy(which, step).wait_send()
     for slot in range(4):
 
         @pl.when(owner(slot) != me)
         def _():
             for copy in part_copies(slot):
                 copy.wait_send()
+    for which in range(2):
+        keep_copy(which).wait()
+    for which in range(2):
+        for step in range(1, N_TP):
+            tp_copy(which, step).wait_send()
+
+        def sent(step, _):
+            page_copy(which, step).wait_send()
+            return 0
+
+        lax.fori_loop(1, N_SEQ, sent, 0)
+    for other_y in range(4):
+
+        @pl.when(q_dest(other_y) != me)
+        def _():
+            q_remote(other_y).wait_send()
+
+    for side in range(2):
+
+        @pl.when(home + side != me)
+        def _():
+            f_remote(side).wait_send()
+
+
+def hand_out_kernel(key_in, value_in, attended_in, key_out, value_out, attended_out):
+    key_out[...] = key_in[...]
+    value_out[...] = value_in[...]
+    attended_out[...] = attended_in[...]
 
 
 def on_device(
@@ -609,23 +616,26 @@
     w_value,
     queries,
 ):
-    rates = frequencies()
-    rates = jnp.concatenate([rates, rates])[None, :]
+    rates = jnp.asarray(frequencies())
     vmem = pl.BlockSpec(memory_space=pltpu.VMEM)
     smem = pl.BlockSpec(memory_space=pltpu.SMEM)
-    hbm = pl.BlockSpec(memory_space=pl.ANY)
+    hbm = pl.BlockSpec(memory_space=pltpu.HBM)
     bf16 = jnp.bfloat16
     dma = pltpu.SemaphoreType.DMA
-    key_cache, value_cache, q_group = pl.pallas_call(
-        exchange_kernel,
-        out_shape=[
-            jax.ShapeDtypeStruct((TOK_DEV, WIDTH), bf16),
-            jax.ShapeDtypeStruct((TOK_DEV, WIDTH), bf16),
-            jax.ShapeDtypeStruct((4, HEADS, BLOCK, HD), bf16),
-        ],
-        in_specs=[smem, vmem, smem, smem, vmem, hbm, hbm, hbm, hbm, hbm, vmem],
-        out_specs=[vmem, vmem, hbm],
+    results = [
+        jax.ShapeDtypeStruct((TOK_DEV, WIDTH), bf16),
+        jax.ShapeDtypeStruct((TOK_DEV, WIDTH), bf16),
+        jax.ShapeDtypeStruct((BLOCK, HEADS * HD), bf16),
+    ]
+    made = pl.pallas_call(
+        blend_kernel,
+        out_shape=results,
+        in_specs=[smem, hbm, smem, smem, vmem, hbm, hbm, hbm, hbm, hbm, hbm],
+        out_specs=[hbm, hbm, vmem],
         scratch_shapes=[
+            pltpu.VMEM((BLOCK, HEADS * HD), bf16),
+            pltpu.VMEM((32, HD), jnp.int32),
+            pltpu.VMEM((4, HEADS, BLOCK, HD), bf16),
             pltpu.VMEM((128, PAGE, WIDTH), bf16),
             pltpu.VMEM((128, PAGE, WIDTH), bf16),
             pltpu.VMEM((2, N_SEQ, CAP, PAGE, WIDTH), bf16),
@@ -643,32 +653,6 @@
             pltpu.VMEM((8, HD), jnp.int32),
             pltpu.SMEM((PASSAGES, HD), jnp.int32),
             pltpu.SMEM((8, HD), jnp.int32),
-            dma((2,)),
-            dma((5,)),
-            dma((2, N_TP)),
-            dma((2, N_TP)),
-            dma((2, N_SEQ)),
-            dma((2, N_SEQ)),
-            dma((4,)),
-            dma((4,)),
-            dma((2,)),
-            dma((2,)),
-        ],
-        compiler_params=pltpu.CompilerParams(
-            collective_id=0, has_side_effects=True, vmem_limit_bytes=48 * 2**20
-        ),
-        name="exchange",
-    )(
-        passage_ids, page_slot, offsets, recompute_blocks, rates,
-        pool_keys, pool_values, hidden_rows, w_key, w_value, queries,
-    )
-
-    attended = pl.pallas_call(
-        attend_kernel,
-        out_shape=jax.ShapeDtypeStruct((BLOCK, HEADS * HD), bf16),
-        in_specs=[smem, hbm, hbm, vmem],
-        out_specs=vmem,
-        scratch_shapes=[
             pltpu.VMEM((4, 2, TOK_DEV, WIDTH), bf16),
             pltpu.VMEM((4, 2, TOK_DEV, WIDTH), bf16),
             pltpu.VMEM((4, HEADS, BLOCK, 2 * HD), jnp.float32),
@@ -678,6 +662,16 @@
             pltpu.VMEM((4, HEADS, BLOCK, HD), bf16),
             pltpu.VMEM((4, BLOCK, HD), jnp.float32),
             dma((2,)),
+            dma((7,)),
+            dma((2, N_TP)),
+            dma((2, N_TP)),
+            dma((2, N_SEQ)),
+            dma((2, N_SEQ)),
+            dma((4,)),
+            dma((4,)),
+            dma((2,)),
+            dma((2,)),
+            dma((2,)),
             dma((2, 4)),
             dma((2, 4)),
             dma((2, 4)),
@@ -686,11 +680,24 @@
             dma((2, 4)),
         ],
         compiler_params=pltpu.CompilerParams(
-            collective_id=1, has_side_effects=True, vmem_limit_bytes=56 * 2**20
+            collective_id=0, has_side_effects=True, vmem_limit_bytes=60 * 2**20
         ),
-        name="attend",
-    )(recompute_blocks, key_cache, value_cache, q_group)
-    return (key_cache, value_cache, attended)
+        name="blend_and_attend",
+    )(
+        passage_ids, page_slot, offsets, recompute_blocks.reshape(-1), rates,
+        pool_keys, pool_values, hidden_rows, w_key, w_value, queries,
+    )
+    slabs = [pl.BlockSpec((r.shape[0] // 2, r.shape[1]), lambda i: (i, 0)) for r in results]
+    return tuple(
+        pl.pallas_call(
+            hand_out_kernel,
+            out_shape=results,
+            grid=(2,),
+            in_specs=slabs,
+            out_specs=slabs,
+            name="hand_out",
+        )(*made)
+    )
 
 
 def solution(mesh):

time: 181 us -> 166 us (0.917)
  local copies, waits for them, and re-layouts: 13.7 us -> 1.36 us
  Pallas kernels: 166 us -> 163 us
    unnamed x26 -> x1, local copies, waits for them, and re-layouts: 13.7 us -> 0.76 us
    pallas_call x2, Pallas kernels: 166 us -> 163 us  [the longest x1 161 us: on_device(): pl.pallas_call(blend_kernel, out_shape=results, in_specs=[smem, hbm, smem...]
where the time goes in v3:
time: 166 us; the launch traced here: 165 us
  Pallas kernels  163 us (98%)
    pallas_call x1, Pallas kernels, on_device(): pl.pallas_call(blend_kernel, out_shape=results, in_specs=[smem, hbm, smem...  161 us

profile of v3, /device:TPU:121, one launch (start us, length us, event | category | flops | bytes accessed | tf_op | source)
XLA Modules:
  0.0 165.2 jit_solution(17906564216946076538)
XLA Ops:
  0.6 0.8 copy.15
  1.4 0.6 reshape.9.recompute_blocks
  2.0 160.9 %blend_and_attend.1 = (bf16[1024,256]{1,0:T(8,128)(2,1)}, bf16[1024,256]{1,0:T(8,128)(2,1)}, bf16[128,2048]{1,0:T(8,128)(2,1)}) custom-call(s32[16]{0:T(128)} %passage_ids.1, s32[32,128]{1,0:T(8,128)} %page_slot.1, s32[16]{0:T(128)} %offsets.1, s32[32]{0:T(128)} %reshape.9.recompute_blocks, f32[1,128]{1,0:T(1,128)} %constant.2.clone.rates, ...), custom_call_target="tpu_custom_call" | custom-call | tf_op jit(solution)/shard_map/blend_and_attend/pallas_call | solution.py:630
  162.9 2.3 %hand_out.1 = (bf16[1024,256]{1,0:T(8,128)(2,1)}, bf16[1024,256]{1,0:T(8,128)(2,1)}, bf16[128,2048]{1,0:T(8,128)(2,1)}) custom-call(bf16[1024,256]{1,0:T(8,128)(2,1)} %get-tuple-element.6.key_in, bf16[1024,256]{1,0:T(8,128)(2,1)} %get-tuple-element.7.value_in, bf16[128,2048]{1,0:T(8,128)(2,1)} %get-tuple-element.8.attended_in), custom_call_target="tpu_custom_call" | custom-call | tf_op jit(solution)/shard_map/hand_out/pallas_call | solution.py:692

commit v4 on v3

--- a/solution.py
+++ b/solution.py
@@ -79,10 +79,10 @@
 def blend_kernel(
     passage_ids, page_slot, offsets, recompute_blocks, rates,
     pool_k, pool_v, hidden, w_key, w_value, queries,
-    out_k, out_v, out_ref,
+    out_k, out_v, part_in, stat_in,
     query_buf, slot_buf, q_group, rows_k, rows_v, outgoing, arriving_k, arriving_v, turned, fresh, fresh_in,
     hidden_buf, w_buf, t_cos, t_sin, used, send_tab, arrival_tab, send_index, arrival,
-    k_buf, v_buf, acc, peak, part, stat, part_in, stat_in,
+    k_buf, v_buf, acc, peak, part, stat,
     own_sem, load_sem, tp_send, tp_recv, page_send, page_recv, q_send, q_recv, f_send, f_recv,
     out_sem, kv_send, kv_recv, side_send, side_recv, part_send, part_recv,
 ):
@@ -227,15 +227,24 @@
     def f_local():
         return pltpu.make_async_copy(fresh, fresh_in.at[which_block], f_recv.at[which_block])
 
+    far = lax.rem(y + 2, 4)
+
+    def q_start(other_y):
+        @pl.when(q_dest(other_y) != me)
+        def _():
+            q_remote(other_y).start()
+
+        @pl.when(q_dest(other_y) == me)
+        def _():
+            q_local().start()
+
     for other_y in range(4):
 
-        @pl.when(q_dest(other_y) != me)
-        def _():
-            q_remote(other_y).start()
-
-        @pl.when(q_dest(other_y) == me)
-        def _():
-            q_local().start()
+        @pl.when(far != other_y)
+        def _():
+            q_start(other_y)
+
+    tp_start(1)
 
     loads[4].wait()
     for row in range(PASSAGES):
@@ -327,27 +336,38 @@
                 device_id_type=MESH,
             ).wait_recv()
         own_copy(which).wait()
-        if which == 0:
-            tp_start(1)
-
-        def pick(step, _):
+
+        def pick(step):
             peer = lax.rem(me + step, N_SEQ)
             for rank in range(CAP):
                 outgoing[which, peer, rank] = rows[which][
                     send_index[peer // 2, lax.rem(peer, 2) * CAP + rank]
                 ]
 
-            @pl.when(step > 0)
-            def _():
+        def pick_and_send(part, _):
+            for number in range(5):
+                step = part * 5 + number + 1
+                pick(step)
                 page_copy(which, step).start()
-
             return 0
 
-        lax.fori_loop(0, N_SEQ, pick, 0)
+        lax.fori_loop(0, 6, pick_and_send, 0)
+        pick(31)
+        page_copy(which, 31).start()
+        pick(0)
         arriving[which][me] = outgoing[which, me]
 
+    q_start(far)
+
+    def q_landed(slot):
+        return on_seq(turned, q_group.at[slot], q_send.at[0], q_recv.at[slot], me)
+
     for slot in range(4):
-        on_seq(turned, q_group.at[slot], q_send.at[0], q_recv.at[slot], me).wait_recv()
+
+        @pl.when(far != slot)
+        def _():
+            q_landed(slot).wait_recv()
+
     for slot in range(2):
         on_seq(fresh, fresh_in.at[slot], f_send.at[0], f_recv.at[slot], me).wait_recv()
 
@@ -395,6 +415,11 @@
     ones = jnp.ones((PASSAGE_LEN, HD), jnp.bfloat16)
 
     def fold(slot, level, limit):
+        if limit is not None:
+            shape = (QT, PASSAGE_LEN)
+            ahead = lax.broadcasted_iota(jnp.int32, shape, 1) - (
+                lax.broadcasted_iota(jnp.int32, shape, 0) & (BLOCK - 1)
+            )
         for index in range(8 // UNIT):
             for kv in range(2):
                 cols = slice(kv * HD, (kv + 1) * HD)
@@ -404,10 +429,7 @@
                 values = v_buf[level].reshape(PASSAGE_LEN, WIDTH)[:, cols]
                 score = lax.dot_general(q, keys, BY_KEY, preferred_element_type=jnp.float32)
                 if limit is not None:
-                    token = lax.broadcasted_iota(jnp.int32, score.shape, 1)
-                    row = lax.broadcasted_iota(jnp.int32, score.shape, 0) % BLOCK + limit
-                    allowed = token <= row
-                    score = jnp.where(allowed, score, MASKED)
+                    score = jnp.where(ahead <= limit, score, MASKED)
                 old = peak[slot, heads].reshape(QT, HD)
                 new = jnp.maximum(old, jnp.max(score, axis=1, keepdims=True))
                 keep = jnp.exp2((old - new) * EXPONENT)
@@ -482,6 +504,16 @@
     def ranked(order):
         return 2 * lax.rem(order, 2) + lax.rem(order // 2 + group, 2)
 
+    far_order = sum(jnp.where(ranked(3 - order) == far, order, 0) for order in range(4))
+    soon = jnp.where((z == 1) | (z == 2), 1, 3)
+    later = 4 - soon
+
+    def sees(slot, level):
+        return slot_passage(slot) >= level * 4 + y
+
+    def unfinished(slot):
+        return sees(slot, near(4 - later)) | sees(slot, near(2))
+
     def arrive(turn_index, _):
         @pl.when(turn_index == 0)
         def _():
@@ -495,22 +527,14 @@
             kv_landed(0, 3).wait_recv()
             side_copy(0, 3).start()
             for which in range(2):
-                side_landed(which, 1).wait_recv()
+                side_landed(which, soon).wait_recv()
 
         @pl.when(turn_index == 2)
-        def _():
-            for which in range(2):
-                side_landed(which, 3).wait_recv()
-
-        step = jnp.where(turn_index < 2, turn_index, 5 - turn_index)
-        level = near(4 - step)
-
-        @pl.when(turn_index == 3)
         def _():
             def early(order, _):
                 slot = ranked(order)
 
-                @pl.when(slot_passage(slot) < level * 4 + y)
+                @pl.when(jnp.logical_not(unfinished(slot)))
                 def _():
                     give_back(slot)
 
@@ -520,48 +544,55 @@
             for which in range(2):
                 kv_landed(which, 2).wait_recv()
                 side_copy(which, 2).start()
+                side_landed(which, later).wait_recv()
             for which in range(2):
                 side_landed(which, 2).wait_recv()
 
         def each(order, _):
-            slot = ranked(jnp.where(turn_index == 3, order, 3 - order))
-            visit(slot, level)
+            skip = jnp.where((turn_index == 0) & (order >= far_order), 1, 0)
+            picked = ranked(jnp.where(turn_index == 2, order // 2, 3 - lax.rem(order + skip, 4)))
+            last = (turn_index == 0) & (order == 3)
+            slot = jnp.where(last, far, picked)
+            step = jnp.where(
+                turn_index == 2,
+                jnp.where(lax.rem(order, 2) == 0, later, 2),
+                jnp.where(turn_index == 1, soon, 0),
+            )
+
+            @pl.when(last)
+            def _():
+                q_landed(far).wait_recv()
+
+            visit(slot, near(4 - step))
 
             @pl.when((turn_index == 0) & (order == 1))
             def _():
-                for which, early_step in ((0, 1), (1, 3)):
-                    kv_landed(which, early_step).wait_recv()
-                    pass_on(which).start()
-                    side_copy(which, early_step).start()
-
-            @pl.when((turn_index == 3) & (slot_passage(slot) >= level * 4 + y))
+                kv_landed(0, 1).wait_recv()
+                pass_on(0).start()
+                side_copy(0, 1).start()
+
+            @pl.when((turn_index == 0) & (order == 3))
+            def _():
+                kv_landed(1, 3).wait_recv()
+                pass_on(1).start()
+                side_copy(1, 3).start()
+
+            @pl.when((turn_index == 2) & (lax.rem(order, 2) == 1) & unfinished(slot))
             def _():
                 give_back(slot)
 
             return 0
 
-        lax.fori_loop(0, 4, each, 0)
+        lax.fori_loop(0, jnp.where(turn_index == 2, 8, 4), each, 0)
         return 0
 
-    lax.fori_loop(0, 4, arrive, 0)
+    lax.fori_loop(0, 3, arrive, 0)
 
     for slot in range(4):
         on_seq(part.at[0], part_in.at[slot], part_send.at[0, 0], part_recv.at[0, slot],
                me).wait_recv()
         on_seq(stat.at[0], stat_in.at[slot], part_send.at[1, 0], part_recv.at[1, slot],
                me).wait_recv()
-    logs = [stat_in[slot] for slot in range(4)]
-    top = jnp.maximum(jnp.maximum(logs[0], logs[1]), jnp.maximum(logs[2], logs[3]))
-    shares = [jnp.exp2(log - top) for log in logs]
-    whole = 1.0 / (shares[0] + shares[1] + shares[2] + shares[3])
-    shares = [share * whole for share in shares]
-    for head in range(HEADS):
-        result = sum(
-            part_in[slot, head].astype(jnp.float32) * shares[slot][:, head : head + 1]
-            for slot in range(4)
-        )
-        out_ref[:, head * HD : (head + 1) * HD] = result.astype(jnp.bfloat16)
-
     for which in range(2):
         for step in (1, 3):
             kv_copy(which, step).wait_send()
@@ -598,10 +629,23 @@
             f_remote(side).wait_send()
 
 
-def hand_out_kernel(key_in, value_in, attended_in, key_out, value_out, attended_out):
+def merge_kernel(key_in, value_in, parts, stats, key_out, value_out, attended):
     key_out[...] = key_in[...]
     value_out[...] = value_in[...]
-    attended_out[...] = attended_in[...]
+    logs = [stats[slot] for slot in range(4)]
+    top = jnp.maximum(jnp.maximum(logs[0], logs[1]), jnp.maximum(logs[2], logs[3]))
+    shares = [jnp.exp2(log - top) for log in logs]
+    whole = 1.0 / (shares[0] + shares[1] + shares[2] + shares[3])
+    shares = [share * whole for share in shares]
+    lane = lax.broadcasted_iota(jnp.int32, (BLOCK, HD), 1)
+    for index in range(HEADS // 2):
+        mine = lane == pl.program_id(0) * (HEADS // 2) + index
+        result = sum(
+            parts[slot, index].astype(jnp.float32)
+            * jnp.sum(jnp.where(mine, shares[slot], 0.0), axis=1, keepdims=True)
+            for slot in range(4)
+        )
+        attended[:, index * HD : (index + 1) * HD] = result.astype(jnp.bfloat16)
 
 
 def on_device(
@@ -622,16 +666,17 @@
     hbm = pl.BlockSpec(memory_space=pltpu.HBM)
     bf16 = jnp.bfloat16
     dma = pltpu.SemaphoreType.DMA
-    results = [
-        jax.ShapeDtypeStruct((TOK_DEV, WIDTH), bf16),
-        jax.ShapeDtypeStruct((TOK_DEV, WIDTH), bf16),
-        jax.ShapeDtypeStruct((BLOCK, HEADS * HD), bf16),
-    ]
+    cache = jax.ShapeDtypeStruct((TOK_DEV, WIDTH), bf16)
     made = pl.pallas_call(
         blend_kernel,
-        out_shape=results,
+        out_shape=[
+            cache,
+            cache,
+            jax.ShapeDtypeStruct((4, HEADS, BLOCK, HD), bf16),
+            jax.ShapeDtypeStruct((4, BLOCK, HD), jnp.float32),
+        ],
         in_specs=[smem, hbm, smem, smem, vmem, hbm, hbm, hbm, hbm, hbm, hbm],
-        out_specs=[hbm, hbm, vmem],
+        out_specs=[hbm, hbm, hbm, hbm],
         scratch_shapes=[
             pltpu.VMEM((BLOCK, HEADS * HD), bf16),
             pltpu.VMEM((32, HD), jnp.int32),
@@ -657,8 +702,6 @@
             pltpu.VMEM((4, 2, TOK_DEV, WIDTH), bf16),
             pltpu.VMEM((4, HEADS, BLOCK, 2 * HD), jnp.float32),
             pltpu.VMEM((4, HEADS, BLOCK, HD), jnp.float32),
-            pltpu.VMEM((4, HEADS, BLOCK, HD), bf16),
-            pltpu.VMEM((4, BLOCK, HD), jnp.float32),
             pltpu.VMEM((4, HEADS, BLOCK, HD), bf16),
             pltpu.VMEM((4, BLOCK, HD), jnp.float32),
             dma((2,)),
@@ -687,15 +730,20 @@
         passage_ids, page_slot, offsets, recompute_blocks.reshape(-1), rates,
         pool_keys, pool_values, hidden_rows, w_key, w_value, queries,
     )
-    slabs = [pl.BlockSpec((r.shape[0] // 2, r.shape[1]), lambda i: (i, 0)) for r in results]
+    slab = pl.BlockSpec((TOK_DEV // 2, WIDTH), lambda i: (i, 0))
     return tuple(
         pl.pallas_call(
-            hand_out_kernel,
-            out_shape=results,
+            merge_kernel,
+            out_shape=[cache, cache, jax.ShapeDtypeStruct((BLOCK, HEADS * HD), bf16)],
             grid=(2,),
-            in_specs=slabs,
-            out_specs=slabs,
-            name="hand_out",
+            in_specs=[
+                slab,
+                slab,
+                pl.BlockSpec((4, HEADS // 2, BLOCK, HD), lambda i: (0, i, 0, 0)),
+                pl.BlockSpec((4, BLOCK, HD), lambda i: (0, 0, 0)),
+            ],
+            out_specs=[slab, slab, pl.BlockSpec((BLOCK, HEADS * HD // 2), lambda i: (0, i))],
+            name="merge",
         )(*made)
     )
 

time: 166 us -> 160 us (0.964)
  Pallas kernels: 163 us -> 158 us
    pallas_call x2, Pallas kernels: 163 us -> 158 us  [the longest x1 154 us: on_device(): pl.pallas_call(blend_kernel, out_shape=[cache, cache, jax.ShapeDtypeStruc...]
where the time goes in v4:
time: 160 us
  Pallas kernels  158 us (99%)
    pallas_call x1, Pallas kernels, on_device(): pl.pallas_call(blend_kernel, out_shape=[cache, cache, jax.ShapeDtypeStruc...  154 us
    pallas_call x1, Pallas kernels, on_device(): pl.pallas_call(merge_kernel, out_shape=[cache, cache, jax.ShapeDtypeStruc...  3.72 us

profile of v4, /device:TPU:121, one launch (start us, length us, event | category | flops | bytes accessed | tf_op | source)
XLA Modules:
  0.0 160.0 jit_solution(16650214120450711611)
XLA Ops:
  0.6 0.8 copy.15
  1.4 0.6 reshape.9.recompute_blocks
  2.0 154.3 %blend_and_attend.1 = (bf16[1024,256]{1,0:T(8,128)(2,1)}, bf16[1024,256]{1,0:T(8,128)(2,1)}, bf16[4,16,128,128]{3,2,1,0:T(8,128)(2,1)}, f32[4,128,128]{2,1,0:T(8,128)}) custom-call(s32[16]{0:T(128)} %passage_ids.1, s32[32,128]{1,0:T(8,128)} %page_slot.1, s32[16]{0:T(128)} %offsets.1, s32[32]{0:T(128)} %reshape.9.recompute_blocks, ...), custom_call_target="tpu_custom_call" | custom-call | tf_op jit(solution)/shard_map/blend_and_attend/pallas_call | solution.py:670
  156.3 3.7 %merge.1 = (bf16[1024,256]{1,0:T(8,128)(2,1)}, bf16[1024,256]{1,0:T(8,128)(2,1)}, bf16[128,2048]{1,0:T(8,128)(2,1)}) custom-call(bf16[1024,256]{1,0:T(8,128)(2,1)} %get-tuple-element.7.key_in, bf16[1024,256]{1,0:T(8,128)(2,1)} %get-tuple-element.8.value_in, bf16[4,16,128,128]{3,2,1,0:T(8,128)(2,1)} %get-tuple-element.9.parts, ...), custom_call_target="tpu_custom_call" | custom-call | tf_op jit(solution)/shard_map/merge/pallas_call | solution.py:735

commit v5 on v4

--- a/solution.py
+++ b/solution.py
@@ -115,7 +115,7 @@
 
     loads[3].wait()
     my_passage = lax.rem(me, PASSAGES)
-    my_start = recompute_blocks[my_passage * RB + me // PASSAGES] * BLOCK
+    my_start = recompute_blocks[me // PASSAGES, my_passage] * BLOCK
     q_cos, q_sin = rotation(offsets[my_passage] + my_start, BLOCK, rates[...])
     for head in range(HEADS):
         cols = slice(head * HD, (head + 1) * HD)
@@ -388,7 +388,7 @@
 
         def put(index, _):
             block = core * 8 + index
-            first, second = (recompute_blocks[me // 2 * RB + number] for number in range(RB))
+            first, second = (recompute_blocks[number, me // 2] for number in range(RB))
             here = jnp.full((PAGE, WIDTH), block, jnp.int32)
             flag = (here == first) | (here == second)
             for page in range(8):
@@ -456,7 +456,7 @@
 
         @pl.when(passage == mine)
         def _():
-            fold(slot, level, recompute_blocks[mine * RB + home_level(z, core, slot) // 2] * BLOCK)
+            fold(slot, level, recompute_blocks[home_level(z, core, slot) // 2, mine] * BLOCK)
 
     def owner(slot):
         return home_level(z, core, slot) * 8 + slot * 2 + core
@@ -514,6 +514,17 @@
     def unfinished(slot):
         return sees(slot, near(4 - later)) | sees(slot, near(2))
 
+    def hand_over(step):
+        @pl.when(step == 1)
+        def _():
+            kv_landed(1, 1).wait_recv()
+            side_copy(1, 1).start()
+
+        @pl.when(step == 3)
+        def _():
+            kv_landed(0, 3).wait_recv()
+            side_copy(0, 3).start()
+
     def arrive(turn_index, _):
         @pl.when(turn_index == 0)
         def _():
@@ -522,10 +533,7 @@
 
         @pl.when(turn_index == 1)
         def _():
-            kv_landed(1, 1).wait_recv()
-            side_copy(1, 1).start()
-            kv_landed(0, 3).wait_recv()
-            side_copy(0, 3).start()
+            hand_over(soon)
             for which in range(2):
                 side_landed(which, soon).wait_recv()
 
@@ -564,6 +572,10 @@
                 q_landed(far).wait_recv()
 
             visit(slot, near(4 - step))
+
+            @pl.when((turn_index == 1) & (order == 1))
+            def _():
+                hand_over(later)
 
             @pl.when((turn_index == 0) & (order == 1))
             def _():
@@ -727,7 +739,7 @@
         ),
         name="blend_and_attend",
     )(
-        passage_ids, page_slot, offsets, recompute_blocks.reshape(-1), rates,
+        passage_ids, page_slot, offsets, recompute_blocks.T, rates,
         pool_keys, pool_values, hidden_rows, w_key, w_value, queries,
     )
     slab = pl.BlockSpec((TOK_DEV // 2, WIDTH), lambda i: (i, 0))

time: 160 us -> 158 us (0.988)
  no operation moved by 1% of the time
where the time goes in v5:
time: 158 us
  Pallas kernels  158 us (100%)
    pallas_call x1, Pallas kernels, on_device(): pl.pallas_call(blend_kernel, out_shape=[cache, cache, jax.ShapeDtypeStruc...  154 us
    pallas_call x1, Pallas kernels, on_device(): pl.pallas_call(merge_kernel, out_shape=[cache, cache, jax.ShapeDtypeStruc...  3.72 us

profile of v5, /device:TPU:121, one launch (start us, length us, event | category | flops | bytes accessed | tf_op | source)
XLA Modules:
  0.0 158.2 jit_solution(13737209856087632026)
XLA Ops:
  0.6 153.9 %blend_and_attend.1 = (bf16[1024,256]{1,0:T(8,128)(2,1)}, bf16[1024,256]{1,0:T(8,128)(2,1)}, bf16[4,16,128,128]{3,2,1,0:T(8,128)(2,1)}, f32[4,128,128]{2,1,0:T(8,128)}) custom-call(s32[16]{0:T(128)} %passage_ids.1, s32[32,128]{1,0:T(8,128)} %page_slot.1, s32[16]{0:T(128)} %offsets.1, s32[2,16]{1,0:T(2,128)} %bitcast.1, f32[1,128]{1,0:T(1,128)} %constant.2.clone.rates, ...), custom_call_target="tpu_custom_call" | custom-call | tf_op jit(solution)/shard_map/blend_and_attend/pallas_call | solution.py:682
  154.5 3.7 %merge.1 = (bf16[1024,256]{1,0:T(8,128)(2,1)}, bf16[1024,256]{1,0:T(8,128)(2,1)}, bf16[128,2048]{1,0:T(8,128)(2,1)}) custom-call(bf16[1024,256]{1,0:T(8,128)(2,1)} %get-tuple-element.7.key_in, bf16[1024,256]{1,0:T(8,128)(2,1)} %get-tuple-element.8.value_in, bf16[4,16,128,128]{3,2,1,0:T(8,128)(2,1)} %get-tuple-element.9.parts, ...), custom_call_target="tpu_custom_call" | custom-call | tf_op jit(solution)/shard_map/merge/pallas_call | solution.py:747
